TPU v7x, 256 devices: a whole 4x4x8 slice. The times are simulated.
256 devices in a mesh: dp: 32 (over x, y, core), expert: 8 (over z).
Axes of the slice: x: 4, y: 4, z: 8, core: 2. Of those that a mesh axis runs over, the one named last changes fastest.
Arguments:
- tokens: bfloat16 [32768, 4096], P(('dp', 'expert')), may hold values from -6 to 6
- router_weight: float32 [4096, 128], replicated, may hold values from -0.1875 to 0.1875
- rollout_ids: int32 [32768, 8], P(('dp', 'expert')), may hold values from 0 to 127, all different within a row; in each aligned block of 128 rows (0 to 127, 128 to 255, ...) at most 9 rows name the same one
- source_row: int32 [32768], P(('dp', 'expert')), may hold values from 0 to 32767, as said below
- gate_weight: bfloat16 [32, 4096, 1536], P('dp', None, 'expert'), may hold values from -0.09375 to 0.09375
- up_weight: bfloat16 [32, 4096, 1536], P('dp', None, 'expert'), may hold values from -0.09375 to 0.09375
- down_weight: bfloat16 [32, 1536, 4096], P('dp', None, 'expert'), may hold values from -0.15625 to 0.15625
Outputs:
- layer_out: bfloat16 [32768, 4096], P(('dp', 'expert'))
Inputs may be any that keep to these rules, and one draw needn't show every extreme that they name: `rollout_ids`: each row names 8 different experts. In every aligned block of 128 rows no expert is named by more than 9 rows, a bound that some block reaches. `source_row`: A permutation of the 32768 rows. The 128 trainer rows of an aligned block all read rows of one aligned block of 128 rollout rows, the blocks correspond one to one, and a trainer block's index and its rollout block's index are equal modulo 8.
All inputs are finite; a program needn't handle non-finite values.
Results may differ from a plain program's by a relative error of at most 0.0058.
Values may be sent and summed in bfloat16 or wider, within the bound.
No kernel may reach another device: no remote copies, remote signals or barrier semaphores. Data moves between devices by JAX's collectives and lax.ppermute only.
A program may use at most 128 MiB of HBM per device.

v0:
```python
import jax
import jax.numpy as jnp
from jax import lax
from jax.sharding import PartitionSpec as P


def per_device(tokens, router_weight, rollout_ids, source_row, gate_weight, up_weight, down_weight):
    owners = lax.axis_size("dp")
    columns = lax.axis_size("expert")
    tok_rows, model_width = tokens.shape
    top_count = rollout_ids.shape[1]
    capacity = tok_rows * top_count // router_weight.shape[1] + 1
    slot_rows = owners * capacity
    blocks = lax.all_gather(rollout_ids, "dp", axis=0, tiled=True)
    local_row = source_row // tok_rows // columns * tok_rows + source_row % tok_rows
    expert_ids = jnp.take(blocks, local_row, axis=0)
    logits = jnp.dot(tokens.astype(jnp.float32), router_weight, precision=lax.Precision.HIGHEST)
    picked = jnp.take_along_axis(logits, expert_ids, axis=1)
    raised = jnp.exp(picked)
    weights = raised / jnp.sum(raised, axis=1, keepdims=True)
    owner_iota = jnp.arange(owners, dtype=jnp.int32)
    matches = expert_ids[:, :, None] == owner_iota[None, None, :]
    pick_weight = jnp.sum(jnp.where(matches, weights[:, :, None], 0.0), axis=1)
    chosen = jnp.sum(matches.astype(jnp.int32), axis=1)
    slot_rank = jnp.cumsum(chosen, axis=0) - chosen
    slot_iota = jnp.arange(capacity, dtype=jnp.int32)
    selector = (chosen[:, :, None] == 1) & (slot_rank[:, :, None] == slot_iota[None, None, :])
    selector = selector.reshape(tok_rows, slot_rows)
    outgoing = jnp.einsum(
        "ts,td->sd", selector.astype(jnp.bfloat16), tokens, preferred_element_type=jnp.float32
    )
    outgoing = outgoing.astype(jnp.bfloat16)
    arrived = lax.all_to_all(outgoing, "dp", split_axis=0, concat_axis=0, tiled=True)
    gate_part = gate_weight[0]
    up_part = up_weight[0]
    down_part = down_weight[0]
    gathered = lax.all_gather(arrived, "expert", axis=0, tiled=True)
    gate_val = jnp.dot(gathered, gate_part, preferred_element_type=jnp.float32)
    upward = jnp.dot(gathered, up_part, preferred_element_type=jnp.float32)
    hidden = (jax.nn.silu(gate_val) * upward).astype(jnp.bfloat16)
    full_hidden = lax.all_gather(hidden, "expert", axis=1, tiled=True)
    expert_out = jnp.dot(full_hidden, down_part, preferred_element_type=jnp.float32).astype(
        jnp.bfloat16
    )
    out_blocks = expert_out.reshape(columns, slot_rows, expert_out.shape[1])
    sectioned = lax.all_to_all(out_blocks, "expert", split_axis=0, concat_axis=2, tiled=True)
    returned = lax.all_to_all(sectioned, "dp", split_axis=1, concat_axis=1, tiled=True)
    returned = returned.reshape(slot_rows, model_width)
    combine_mat = jnp.where(
        selector.reshape(tok_rows, owners, capacity), pick_weight[:, :, None], 0.0
    )
    combine_mat = combine_mat.reshape(tok_rows, slot_rows)
    layer_out = jnp.dot(combine_mat, returned.astype(jnp.float32), precision=lax.Precision.HIGHEST)
    return layer_out.astype(jnp.bfloat16)


def solution(mesh):
    in_specs = (
        P(("dp", "expert"), None),
        P(),
        P(("dp", "expert"), None),
        P(("dp", "expert")),
        P("dp", None, "expert"),
        P("dp", None, "expert"),
        P("dp", None, "expert"),
    )
    out_specs = P(("dp", "expert"), None)
    return jax.shard_map(
        per_device, mesh=mesh, in_specs=in_specs, out_specs=out_specs, check_vma=False
    )
```

profile of v0, /device:TPU:1, one launch (start us, length us, event | category | flops | bytes accessed | tf_op | source)
XLA Modules:
  0.0 581.4 jit_solution(8114573680205851458)
XLA Ops:
  6.5 0.0 copy-start
  6.5 0.0 copy-start.2
  6.5 0.0 all-gather.3.cloned.1.call-start
  6.5 0.8 compare_and_fusion
  7.4 0.9 copy.31
  8.3 29.6 %all_gather.9 = s32[4096,8]{1,0:T(8,128)} all-gather(s32[128,8]{1,0:T(8,128)S(1)} %copy.31), channel_id=1, replica_groups=mesh['dp'=32,'expert'=8] {'dp'}, dimensions={0}, use_global_device_ids=true | all-gather | bytes 135168 | tf_op jit(solution)/shard_map/all_gather | solution.py:14
  37.9 2.2 gather_fusion
  40.2 0.1 fusion.14
  40.3 0.1 reshape.186
  40.4 0.0 copy-done
  40.4 0.0 copy-done.2
  40.4 1.3 fusion.17
  41.7 6.8 %gather_fusion.1 = f32[1024]{0:T(1024)S(1)} fusion(f32[128,128]{1,0:T(8,128)S(1)} %fusion.17, s32[1024]{0:T(1024)S(1)} %reshape.186), kind=kCustom, calls=%fused_computation.1 | custom fusion | bytes 16384 | tf_op jit(solution)/shard_map/jit(take_along_axis)/gather | solution.py:18
  48.5 0.1 reshape.189
  48.7 0.1 copy.33
  48.8 0.2 reduce_window_sum.11
  49.0 0.1 copy.35
  49.2 0.1 eq.68
  49.3 2.3 convolution_convert_fusion
  51.6 4.6 all_to_all.24
  56.2 55.9 %all_to_all.36 = bf16[32,9,4096]{2,1,0:T(8,128)(2,1)} all-to-all(bf16[32,9,4096]{2,1,0:T(8,128)(2,1)} %all_to_all.24), channel_id=1, replica_groups=mesh['dp'=32,'expert'=8] {'dp'}, dimensions={0} | all-to-all | bytes 4718592 | tf_op jit(solution)/shard_map/all_to_all | solution.py:33
  112.1 4.7 all_to_all.26
  116.8 0.0 copy-start.4
  116.8 0.0 all-gather.3.cloned.1.call-update
  116.8 0.2 all-gather.5.cloned.1.call-start
  117.0 191.5 %all-gather.3.cloned.1.call-done = bf16[2304,4096]{1,0:T(8,128)(2,1)} async-done(((bf16[288,4096]{1,0:T(8,128)(2,1)}), bf16[2304,4096]{1,0:T(8,128)(2,1)}) %all-gather.3.cloned.1.call-update) | async-done | bytes 18874384 | tf_op jit(solution)/shard_map/all_gather | solution.py:37
  308.5 0.0 copy-done.4
  308.5 0.0 copy-start.3
  308.5 12.6 %fusion.5 = f32[2304,192]{0,1:T(8,128)S(1)} fusion(bf16[2304,4096]{1,0:T(8,128)(2,1)} %all-gather.3.cloned.1.call-done, bf16[1,4096,192]{1,2,0:T(8,128)(2,1)S(1)} %copy-done.4), kind=kOutput, calls=%fused_computation.11 | convolution fusion | flops 3623878656 | bytes 22216704 | tf_op jit(solution)/shard_map/dot_general | solution.py:38
  321.2 0.0 copy-done.3
  321.2 0.0 copy-start.5
  321.2 8.8 %fusion = bf16[2304,192]{0,1:T(8,128)(2,1)} fusion(bf16[2304,4096]{1,0:T(8,128)(2,1)S(1)} %copy-done.3, f32[2304,192]{0,1:T(8,128)S(1)} %fusion.5, bf16[1,4096,192]{1,2,0:T(8,128)(2,1)} %param.12), kind=kOutput, calls=%fused_computation.6 | convolution fusion | flops 3626532864 | bytes 23101440 | tf_op jit(solution)/shard_map/dot_general | solution.py:39
  330.0 0.0 all-gather.5.cloned.1.call-update
  330.0 80.6 %all-gather.5.cloned.1.call-done = bf16[2304,1536]{0,1:T(8,128)(2,1)} async-done(((bf16[2304,192]{0,1:T(8,128)(2,1)}), bf16[2304,1536]{0,1:T(8,128)(2,1)}) %all-gather.5.cloned.1.call-update) | async-done | bytes 7077904 | tf_op jit(solution)/shard_map/all_gather | solution.py:41
  410.7 0.0 copy-done.5
  410.7 7.1 %convolution_convert_fusion.2 = bf16[2304,512]{1,0:T(8,128)(2,1)S(1)} fusion(bf16[2304,1536]{0,1:T(8,128)(2,1)} %all-gather.5.cloned.1.call-done, bf16[1,1536,512]{2,1,0:T(8,128)(2,1)S(1)} %copy-done.5), kind=kOutput, calls=%fused_computation.4 | convolution fusion | flops 3625058304 | bytes 11010048 | tf_op jit(solution)/shard_map/dot_general | solution.py:42
  417.8 59.2 %all_to_all.37 = bf16[8,288,512]{2,1,0:T(8,128)(2,1)S(1)} all-to-all(bf16[8,288,512]{2,1,0:T(8,128)(2,1)S(1)} %bitcast.42), channel_id=1, replica_groups=mesh['dp'=32,'expert'=8] {'expert'}, dimensions={0} | all-to-all | bytes 4718592 | tf_op jit(solution)/shard_map/all_to_all | solution.py:46
  477.0 2.8 copy.37
  479.7 14.3 %all_to_all.32 = bf16[1,288,4096]{2,0,1:T(2,128)(2,1)} reshape(bf16[1,288,8,512]{3,2,1,0:T(8,128)(2,1)} %copy.37) | data formatting | bytes 4718592 | tf_op jit(solution)/shard_map/all_to_all | solution.py:46
  494.1 0.5 broadcast.222
  494.6 16.4 %reduce = bf16[288,4096]{1,0:T(8,128)(2,1)} reduce(bf16[288,1,4096]{2,1,0:T(2,128)(2,1)} %bitcast.39, bf16[]{:T(256)} %broadcast.222), dimensions={1}, to_apply=%bitcast.30.reduce_sub_computation | reduce | bytes 4718594
  511.0 4.9 reshape.193
  515.9 9.4 %all-to-all-start.2 = ((bf16[32,2,18432]{2,1,0:T(2,128)(2,1)}), bf16[32,2,18432]{2,1,0:T(2,128)(2,1)}, u32[]{:S(2)}, u32[]{:S(2)}) async-start(bf16[32,2,18432]{2,1,0:T(2,128)(2,1)} %reshape.193), calls=%async_computation.2 | async-start | bytes 4718592 | tf_op jit(solution)/shard_map/all_to_all | solution.py:47
  525.3 0.1 fusion.8
  525.4 31.0 %all-to-all-done.2 = bf16[32,2,18432]{2,1,0:T(2,128)(2,1)} async-done(((bf16[32,2,18432]{2,1,0:T(2,128)(2,1)}), bf16[32,2,18432]{2,1,0:T(2,128)(2,1)}, u32[]{:S(2)}, u32[]{:S(2)}) %all-to-all-start.2) | async-done | bytes 2359328 | tf_op jit(solution)/shard_map/all_to_all | solution.py:47
  556.5 0.0 copy-start.1
  556.5 10.8 %reshape.194 = bf16[288,1,4096]{2,1,0:T(2,128)(2,1)} reshape(bf16[32,2,18432]{2,1,0:T(2,128)(2,1)} %all-to-all-done.2) | data formatting | bytes 4718592
  567.3 7.3 %convolution_convert_fusion.1 = bf16[128,4096]{1,0:T(8,128)(2,1)} fusion(f32[128,288]{0,1:T(8,128)S(1)} %select_n.95, bf16[1,288,4096]{2,0,1:T(2,128)(2,1)} %bitcast.40), kind=kOutput, calls=%fused_computation.3 | convolution fusion | flops 1812463616 | bytes 3555328 | tf_op jit(solution)/shard_map/dot_general | solution.py:53
  574.6 0.0 copy-done.1
  (15 shorter events, 0.4 us)
Async XLA Ops:
  6.5 33.9 %copy-start = (f32[4096,128]{1,0:T(8,128)S(1)}, f32[4096,128]{1,0:T(8,128)}, u32[]{:S(2)}) copy-start(f32[4096,128]{1,0:T(8,128)} %param.8) | copy-start | bytes 6291460
  6.5 33.9 %copy-start.2 = (bf16[128,4096]{1,0:T(8,128)(2,1)S(1)}, bf16[128,4096]{1,0:T(8,128)(2,1)}, u32[]{:S(2)}) copy-start(bf16[128,4096]{1,0:T(8,128)(2,1)} %param.7) | copy-start | bytes 3145732
  6.5 302.0 %all-gather.3.cloned.1.call-start = ((), (), s32[]{:S(2)}) async-start(), calls=%async_computation.3 | async-start | bytes 21233664 | tf_op jit(solution)/shard_map/all_gather | solution.py:37
  116.8 191.8 %copy-start.4 = (bf16[1,4096,192]{1,2,0:T(8,128)(2,1)S(1)}, bf16[1,4096,192]{1,2,0:T(8,128)(2,1)}, u32[]{:S(2)}) copy-start(bf16[1,4096,192]{1,2,0:T(8,128)(2,1)} %param.11) | copy-start | bytes 4718596
  116.8 293.9 %all-gather.5.cloned.1.call-start = ((), (), s32[]{:S(2)}) async-start(), calls=%async_computation.4 | async-start | bytes 7962624 | tf_op jit(solution)/shard_map/all_gather | solution.py:41
  308.5 12.6 %copy-start.3 = (bf16[2304,4096]{1,0:T(8,128)(2,1)S(1)}, bf16[2304,4096]{1,0:T(8,128)(2,1)}, u32[]{:S(2)}) copy-start(bf16[2304,4096]{1,0:T(8,128)(2,1)} %all-gather.3.cloned.1.call-done) | copy-start | bytes 56623108
  321.2 89.5 %copy-start.5 = (bf16[1,1536,512]{2,1,0:T(8,128)(2,1)S(1)}, bf16[1,1536,512]{2,1,0:T(8,128)(2,1)}, u32[]{:S(2)}) copy-start(bf16[1,1536,512]{2,1,0:T(8,128)(2,1)} %param.13) | copy-start | bytes 4718596
  515.9 40.6 %all-to-all-start.2 = ((bf16[32,2,18432]{2,1,0:T(2,128)(2,1)}), bf16[32,2,18432]{2,1,0:T(2,128)(2,1)}, u32[]{:S(2)}, u32[]{:S(2)}) async-start(bf16[32,2,18432]{2,1,0:T(2,128)(2,1)} %reshape.193), calls=%async_computation.2 | async-start | bytes 4718592 | tf_op jit(solution)/shard_map/all_to_all | solution.py:47
  556.5 18.1 %copy-start.1 = (f32[4096,128]{1,0:T(8,128)S(1)}, f32[4096,128]{1,0:T(8,128)}, u32[]{:S(2)}) copy-start(f32[4096,128]{1,0:T(8,128)} %param.8) | copy-start | bytes 6291460
Sparse Core Ops, SparseCore 0:
  116.9 191.5 all-gather.2
  330.1 80.4 all-gather.4
where the time goes:
time: 583 us; the launch traced here: 581 us
  waiting for transfers between devices  303 us (52%)
  blocking collectives  145 us (25%)
  local copies, waits for them, and re-layouts  53.3 us (9%)
  matrix products  39.4 us (7%)
  other arithmetic  17.7 us (3%)
  between operations  13.6 us (2%)
  starting transfers between devices  9.58 us (2%)
    all_gather x1, waiting for transfers between devices, per_device(): gathered = lax.all_gather(arrived, 'expert', axis=0, tiled=True)  192 us
    all_gather x1, waiting for transfers between devices, per_device(): full_hidden = lax.all_gather(hidden, 'expert', axis=1, tiled=True)  80.6 us
    all_to_all x1, blocking collectives, per_device(): lax.all_to_all(out_blocks, 'expert', split_axis=0, concat_axis=2, tiled=T...  59.2 us
    all_to_all x1, blocking collectives, per_device(): lax.all_to_all(outgoing, 'dp', split_axis=0, concat_axis=0, tiled=True)  55.9 us
    all_to_all x1, waiting for transfers between devices, per_device(): lax.all_to_all(sectioned, 'dp', split_axis=1, concat_axis=1, tiled=True)  31 us
    all_gather x1, blocking collectives, per_device(): blocks = lax.all_gather(rollout_ids, 'dp', axis=0, tiled=True)  29.6 us
    unnamed x16, local copies, waits for them, and re-layouts  17.2 us
    all_to_all x2, local copies, waits for them, and re-layouts, per_device(): lax.all_to_all(out_blocks, 'expert', split_axis=0, concat_axis=2, tiled=T...  17.1 us
  transfers between devices with their start and end apart: 3, of which 3 were waited for; matrix products, arithmetic and copies ran while one was open for 0% of the time, Pallas kernels for 0%

commit v1 on v0

v1 whole, which is shorter than its diff:
```python
import jax
import jax.numpy as jnp
from jax import lax
from jax.sharding import PartitionSpec as P

MAIN = 8


def per_device(tokens, router_weight, rollout_ids, source_row, gate_weight, up_weight, down_weight):
    owners = lax.axis_size("dp")
    columns = lax.axis_size("expert")
    tok_rows, model_width = tokens.shape
    top_count = rollout_ids.shape[1]
    out_width = down_weight.shape[2]
    bf16, f32 = jnp.bfloat16, jnp.float32

    sent_ids = jnp.broadcast_to(rollout_ids.T[None], (owners, top_count, tok_rows))
    blocks = lax.all_to_all(sent_ids, "dp", split_axis=0, concat_axis=0, tiled=True)
    source_block = source_row[0] // (tok_rows * columns)
    block = lax.dynamic_index_in_dim(blocks, source_block, axis=0, keepdims=False)
    place = (source_row % tok_rows)[None, :] == jnp.arange(tok_rows, dtype=jnp.int32)[:, None]
    expert_ids = jnp.dot(
        block.astype(bf16), place.astype(bf16), preferred_element_type=f32
    ).astype(jnp.int32).T

    logits = jnp.dot(tokens.astype(f32), router_weight, precision=lax.Precision.HIGHEST)
    expert_iota = jnp.arange(router_weight.shape[1], dtype=jnp.int32)
    picks = jnp.any(expert_ids[:, :, None] == expert_iota[None, None, :], axis=1)
    raised = jnp.where(picks, jnp.exp(jnp.where(picks, logits, 0.0)), 0.0)
    weights = raised / jnp.sum(raised, axis=1, keepdims=True)
    pick_weight = weights[:, :owners]
    chosen = picks[:, :owners]
    before = jnp.arange(tok_rows)[:, None] > jnp.arange(tok_rows)[None, :]
    slot_rank = jnp.dot(before.astype(bf16), chosen.astype(bf16), preferred_element_type=f32)
    slot_rank = jnp.where(chosen, slot_rank, -1.0)

    def selector(rank, first, count):
        slots = jnp.arange(first, first + count, dtype=f32)
        return rank[..., :, :, None] == slots

    sel_main = selector(slot_rank, 0, MAIN).reshape(tok_rows, owners * MAIN).astype(bf16)
    sel_last = selector(slot_rank, MAIN, 1).reshape(tok_rows, owners).astype(bf16)

    def dispatch(sel, rows):
        out = lax.dot_general(sel, tokens, (((0,), (0,)), ((), ())), preferred_element_type=f32)
        out = out.astype(bf16).reshape(owners, rows, model_width)
        out = lax.all_to_all(out, "dp", split_axis=0, concat_axis=0, tiled=True)
        return out.reshape(owners * rows, model_width)

    arrived_main = dispatch(sel_main, MAIN)
    arrived_last = dispatch(sel_last, 1)

    info = jnp.concatenate([pick_weight, slot_rank], axis=1)
    infos = lax.all_gather(info, "expert", axis=0)

    gate_part = gate_weight[0]
    up_part = up_weight[0]
    down_part = down_weight[0]

    def expert(arrived):
        rows = lax.all_gather(arrived, "expert", axis=0, tiled=True)
        gate_val = lax.dot_general(gate_part, rows, (((0,), (1,)), ((), ())), preferred_element_type=f32)
        upward = lax.dot_general(up_part, rows, (((0,), (1,)), ((), ())), preferred_element_type=f32)
        hidden = (jax.nn.silu(gate_val) * upward).astype(bf16)
        full = lax.all_gather(hidden, "expert", axis=0, tiled=True)
        return lax.dot_general(
            full, down_part, (((0,), (0,)), ((), ())), preferred_element_type=f32
        ).astype(bf16)

    out_main = expert(arrived_main).reshape(columns, owners, MAIN, out_width)
    out_last = expert(arrived_last).reshape(columns, owners, 1, out_width)

    def give_back(out):
        return lax.all_to_all(out, "dp", split_axis=1, concat_axis=1, tiled=True)

    back_main = give_back(out_main).reshape(columns, owners * MAIN, out_width)
    back_last = give_back(out_last).reshape(columns, owners, out_width)

    weight_all = infos[:, :, :owners]
    rank_all = infos[:, :, owners:]

    def combine(first, count, back):
        mat = jnp.where(selector(rank_all, first, count), weight_all[..., None], 0.0)
        mat = mat.reshape(columns, tok_rows, owners * count)
        high = mat.astype(bf16)
        low = (mat - high.astype(f32)).astype(bf16)
        dims = (((2,), (1,)), ((0,), (0,)))
        return lax.dot_general(high, back, dims, preferred_element_type=f32) + lax.dot_general(
            low, back, dims, preferred_element_type=f32
        )

    part = (combine(0, MAIN, back_main) + combine(MAIN, 1, back_last)).astype(bf16)
    whole = lax.all_to_all(part, "expert", split_axis=0, concat_axis=0, tiled=True)
    return jnp.transpose(whole, (1, 0, 2)).reshape(tok_rows, model_width)


def solution(mesh):
    in_specs = (
        P(("dp", "expert"), None),
        P(),
        P(("dp", "expert"), None),
        P(("dp", "expert")),
        P("dp", None, "expert"),
        P("dp", None, "expert"),
        P("dp", None, "expert"),
    )
    out_specs = P(("dp", "expert"), None)
    return jax.shard_map(
        per_device, mesh=mesh, in_specs=in_specs, out_specs=out_specs, check_vma=False
    )
```

time: 583 us -> 442 us (0.76)
  waiting for transfers between devices: 303 us -> 216 us
  local copies, waits for them, and re-layouts: 53.3 us -> 13.9 us
  blocking collectives: 145 us -> 119 us
  starting transfers between devices: 9.58 us -> 33.1 us
  other arithmetic: 17.7 us -> 2.59 us
    all_gather x2 -> x3, waiting for transfers between devices: 272 us -> 209 us  [the longest x2 171 us: expert(): rows = lax.all_gather(arrived, 'expert', axis=0, tiled=True)]
    all_to_all x2 -> x3, blocking collectives: 115 us -> 75.4 us  [the longest x2 44.9 us: dispatch(): out = lax.all_to_all(out, 'dp', split_axis=0, concat_axis=0, tiled=True)]
    all_to_all x4 -> x1, local copies, waits for them, and re-layouts: 26.4 us -> 2.03 us  [dispatch(): out = lax.all_to_all(out, 'dp', split_axis=0, concat_axis=0, tiled=True)]
    all_to_all x1 -> x3, starting transfers between devices: 9.36 us -> 33 us  [the longest x2 24.4 us: give_back(): return lax.all_to_all(out, 'dp', split_axis=1, concat_axis=1, tiled=True)]
    all_to_all x1 -> x3, waiting for transfers between devices: 31 us -> 7.5 us  [the longest x1 4.28 us: per_device(): lax.all_to_all(sent_ids, 'dp', split_axis=0, concat_axis=0, tiled=True)]
    unnamed x1 -> x0, other arithmetic: 16.4 us -> none
    all_gather x1 -> x2, blocking collectives: 29.6 us -> 43.6 us  [the longest x1 22.3 us: expert(): full = lax.all_gather(hidden, 'expert', axis=0, tiled=True)]
    unnamed x16 -> x21, local copies, waits for them, and re-layouts: 17.2 us -> 3.49 us
  transfers between devices with their start and end apart: 3 -> 6, of which waited for: 3 -> 5; matrix products, arithmetic and copies ran while one was open for 0% -> 10% of each run, Pallas kernels for 0% -> 0%
where the time goes in v1:
time: 442 us
  waiting for transfers between devices  216 us (49%)
  blocking collectives  119 us (27%)
  matrix products  40.8 us (9%)
  starting transfers between devices  33.1 us (7%)
  between operations  15.9 us (4%)
  local copies, waits for them, and re-layouts  13.9 us (3%)
    all_gather x2, waiting for transfers between devices, expert(): rows = lax.all_gather(arrived, 'expert', axis=0, tiled=True)  171 us
    all_to_all x2, blocking collectives, dispatch(): out = lax.all_to_all(out, 'dp', split_axis=0, concat_axis=0, tiled=True)  44.9 us
    all_gather x1, waiting for transfers between devices, expert(): full = lax.all_gather(hidden, 'expert', axis=0, tiled=True)  38.2 us
    all_to_all x1, blocking collectives, per_device(): lax.all_to_all(part, 'expert', split_axis=0, concat_axis=0, tiled=True)  30.5 us
    all_to_all x2, starting transfers between devices, give_back(): return lax.all_to_all(out, 'dp', split_axis=1, concat_axis=1, tiled=True)  24.4 us
    all_gather x1, blocking collectives, expert(): full = lax.all_gather(hidden, 'expert', axis=0, tiled=True)  22.3 us
    all_gather x1, blocking collectives, per_device(): infos = lax.all_gather(info, 'expert', axis=0)  21.3 us
    dot_general x2, matrix products, expert(): lax.dot_general(gate_part, rows, (((0,), (1,)), ((), ())), preferred_elem...  14.1 us
  transfers between devices with their start and end apart: 6, of which 5 were waited for; matrix products, arithmetic and copies ran while one was open for 10% of the time, Pallas kernels for 0%

profile of v1, /device:TPU:1, one launch (start us, length us, event | category | flops | bytes accessed | tf_op | source)
XLA Modules:
  0.0 441.6 jit_solution(9261018053787571266)
XLA Ops:
  6.5 0.0 copy-start
  6.5 1.5 broadcast_in_dim.24
  8.0 8.6 %all-to-all-start = ((s32[32,8,128]{2,1,0:T(8,128)}), s32[32,8,128]{2,1,0:T(8,128)S(1)}, u32[]{:S(2)}, u32[]{:S(2)}) async-start(s32[32,8,128]{2,1,0:T(8,128)} %broadcast_in_dim.24), calls=%async_computation | async-start | bytes 262144 | tf_op jit(solution)/shard_map/all_to_all | solution.py:18
  16.6 0.0 all-gather.6.cloned.1.call-start
  19.3 0.1 eq.94
  19.4 0.7 and_select_fusion
  20.1 4.3 all-to-all-done
  24.3 0.1 convolution_convert_fusion.3
  24.5 0.1 copy.46
  24.6 0.3 fusion.59
  24.8 0.1 copy.48
  25.0 0.1 convolution_select_fusion.1
  25.1 2.0 fusion
  27.1 32.0 %all_to_all.30 = bf16[32,8,4096]{2,1,0:T(8,128)(2,1)} all-to-all(bf16[32,8,4096]{2,1,0:T(8,128)(2,1)S(1)} %fusion), channel_id=1, replica_groups=mesh['dp'=32,'expert'=8] {'dp'}, dimensions={0} | all-to-all | bytes 4194304 | tf_op jit(solution)/shard_map/all_to_all | solution.py:47
  59.1 0.0 copy-start.1
  59.1 0.0 all-gather.6.cloned.1.call-update
  59.1 0.0 all-gather.10.cloned.1.call-start
  59.1 1.1 copy-done.1
  60.3 1.0 fusion.1
  61.3 0.5 broadcast.31
  61.7 1.7 reduce
  63.4 0.9 reshape.60
  64.3 12.9 %all_to_all.31 = bf16[32,2,2048]{2,1,0:T(2,128)(2,1)S(1)} all-to-all(bf16[32,2,2048]{2,1,0:T(2,128)(2,1)} %reshape.60), channel_id=1, replica_groups=mesh['dp'=32,'expert'=8] {'dp'}, dimensions={0} | all-to-all | bytes 524288 | tf_op jit(solution)/shard_map/all_to_all | solution.py:47
  77.2 1.0 reshape.61
  78.2 2.0 copy.57
  80.2 0.0 all-gather.10.cloned.1.call-update
  80.2 0.0 all-gather.8.cloned.1.call-start
  80.3 150.9 %all-gather.6.cloned.1.call-done = bf16[2048,4096]{1,0:T(8,128)(2,1)} async-done(((bf16[256,4096]{1,0:T(8,128)(2,1)}), bf16[2048,4096]{1,0:T(8,128)(2,1)}) %all-gather.6.cloned.1.call-update) | async-done | bytes 16777232 | tf_op jit(solution)/shard_map/all_gather | solution.py:61
  231.1 0.0 copy-start.5
  231.1 0.0 copy-start.6
  231.1 11.1 %convolution_bitcast_fusion.1 = f32[192,2048]{1,0:T(8,128)S(1)} fusion(bf16[2048,4096]{1,0:T(8,128)(2,1)} %all-gather.6.cloned.1.call-done, bf16[1,4096,192]{1,2,0:T(8,128)(2,1)} %param.11), kind=kOutput, calls=%fused_computation.6 | convolution fusion | flops 3221225472 | bytes 19922944 | tf_op jit(solution)/shard_map/dot_general | solution.py:62
  242.2 0.0 copy-done.5
  242.3 0.3 copy-done.6
  242.5 6.7 %fusion.3 = bf16[192,2048]{1,0:T(8,128)(2,1)} fusion(bf16[2048,4096]{1,0:T(8,128)(2,1)S(1)} %copy-done.5, bf16[1,4096,192]{1,2,0:T(8,128)(2,1)S(1)} %copy-done.6, f32[192,2048]{1,0:T(8,128)S(1)} %convolution_bitcast_fusion.1), kind=kOutput, calls=%fused_computation.8 | convolution fusion | flops 3223584768 | bytes 20709376 | tf_op jit(solution)/shard_map/dot_general | solution.py:63
  249.2 0.0 all-gather.8.cloned.1.call-update
  249.2 19.8 %all-gather.10.cloned.1.call-done = bf16[256,1,4096]{2,0,1:T(8,128)(2,1)} async-done(((bf16[32,1,4096]{2,0,1:T(8,128)(2,1)}), bf16[256,1,4096]{2,0,1:T(8,128)(2,1)}) %all-gather.10.cloned.1.call-update) | async-done | bytes 2097168 | tf_op jit(solution)/shard_map/all_gather | solution.py:61
  269.0 0.0 copy-start.3
  269.0 3.0 fusion.24
  272.1 0.0 copy-done.3
  272.1 0.1 copy-done.7
  272.1 0.8 fusion.39
  273.0 22.3 %all_gather.23 = bf16[1536,256]{1,0:T(8,128)(2,1)S(1)} all-gather(bf16[192,256]{1,0:T(8,128)(2,1)S(1)} %fusion.39), channel_id=1, replica_groups=mesh['dp'=32,'expert'=8] {'expert'}, dimensions={0}, use_global_device_ids=true | all-gather | bytes 884736 | tf_op jit(solution)/shard_map/all_gather | solution.py:65
  295.3 0.0 copy-done.4
  295.3 0.6 fusion.21
  295.9 0.8 copy.58
  296.7 16.9 %all-to-all-start.4 = ((bf16[8,32,1,512]{3,0,2,1:T(8,128)(2,1)}), bf16[8,32,1,512]{3,0,2,1:T(8,128)(2,1)S(1)}, u32[]{:S(2)}, u32[]{:S(2)}) async-start(bf16[8,32,1,512]{3,0,2,1:T(8,128)(2,1)} %copy.58), calls=%async_computation.4 | async-start | bytes 524288 | tf_op jit(solution)/shard_map/all_to_all | solution.py:74
  313.7 38.2 %all-gather.8.cloned.1.call-done = bf16[1536,2048]{1,0:T(8,128)(2,1)} async-done(((bf16[192,2048]{1,0:T(8,128)(2,1)}), bf16[1536,2048]{1,0:T(8,128)(2,1)}) %all-gather.8.cloned.1.call-update) | async-done | bytes 6291472 | tf_op jit(solution)/shard_map/all_gather | solution.py:65
  351.8 6.7 %convolution_convert_fusion.2 = bf16[2048,512]{1,0:T(8,128)(2,1)S(1)} fusion(bf16[1536,2048]{1,0:T(8,128)(2,1)} %all-gather.8.cloned.1.call-done, bf16[1,1536,512]{2,1,0:T(8,128)(2,1)} %param.13), kind=kOutput, calls=%fused_computation.4 | convolution fusion | flops 3222274048 | bytes 9961472 | tf_op jit(solution)/shard_map/dot_general | solution.py:66
  358.5 1.6 copy.52
  360.1 0.0 all-to-all-done.4
  360.1 7.5 %all-to-all-start.2 = ((bf16[8,32,8,512]{3,2,0,1:T(8,128)(2,1)}), bf16[8,32,8,512]{3,2,0,1:T(8,128)(2,1)}, u32[]{:S(2)}, u32[]{:S(2)}) async-start(bf16[8,32,8,512]{3,2,0,1:T(8,128)(2,1)} %copy.52), calls=%async_computation.2 | async-start | bytes 4194304 | tf_op jit(solution)/shard_map/all_to_all | solution.py:74
  367.6 0.0 copy-done
  367.6 1.8 fusion.90
  369.4 21.3 %all-gather = f32[1024,64]{0,1:T(8,128)S(1)} all-gather(f32[128,64]{0,1:T(8,128)S(1)} %pad_maximum_fusion), channel_id=2, replica_groups=mesh['dp'=32,'expert'=8] {'expert'}, dimensions={0}, use_global_device_ids=true | all-gather | bytes 294912 | tf_op jit(solution)/shard_map/all_gather | solution.py:54
  390.9 1.8 fusion.61
  392.7 3.2 all-to-all-done.2
  395.9 2.2 fusion.10
  398.1 0.0 copy-start.2
  398.1 2.3 fusion.8
  400.4 0.0 copy-done.2
  400.4 0.6 add_convert_fusion
  401.0 30.5 %all_to_all.32 = bf16[8,128,512]{2,1,0:T(8,128)(2,1)S(1)} all-to-all(bf16[8,128,512]{2,1,0:T(8,128)(2,1)S(1)} %add_convert_fusion), channel_id=1, replica_groups=mesh['dp'=32,'expert'=8] {'expert'}, dimensions={0} | all-to-all | bytes 2097152 | tf_op jit(solution)/shard_map/all_to_all | solution.py:93
  431.5 1.3 copy.60
  432.9 2.3 copy.61
  (9 shorter events, 0.1 us)
Async XLA Ops:
  6.5 361.1 %copy-start = (f32[4096,128]{1,0:T(8,128)S(1)}, f32[4096,128]{1,0:T(8,128)}, u32[]{:S(2)}) copy-start(f32[4096,128]{1,0:T(8,128)} %param.8) | copy-start | bytes 6291460
  8.0 16.3 %all-to-all-start = ((s32[32,8,128]{2,1,0:T(8,128)}), s32[32,8,128]{2,1,0:T(8,128)S(1)}, u32[]{:S(2)}, u32[]{:S(2)}) async-start(s32[32,8,128]{2,1,0:T(8,128)} %broadcast_in_dim.24), calls=%async_computation | async-start | bytes 262144 | tf_op jit(solution)/shard_map/all_to_all | solution.py:18
  16.6 214.5 %all-gather.6.cloned.1.call-start = ((), (), s32[]{:S(2)}) async-start(), calls=%async_computation.6 | async-start | bytes 18874368 | tf_op jit(solution)/shard_map/all_gather | solution.py:61
  59.1 1.2 copy-start.1
  59.1 209.9 %all-gather.10.cloned.1.call-start = ((), (), s32[]{:S(2)}) async-start(), calls=%async_computation.8 | async-start | bytes 2359296 | tf_op jit(solution)/shard_map/all_gather | solution.py:61
  80.2 271.6 %all-gather.8.cloned.1.call-start = ((), (), s32[]{:S(2)}) async-start(), calls=%async_computation.7 | async-start | bytes 7077888 | tf_op jit(solution)/shard_map/all_gather | solution.py:65
  231.1 11.1 %copy-start.5 = (bf16[2048,4096]{1,0:T(8,128)(2,1)S(1)}, bf16[2048,4096]{1,0:T(8,128)(2,1)}, u32[]{:S(2)}) copy-start(bf16[2048,4096]{1,0:T(8,128)(2,1)} %all-gather.6.cloned.1.call-done) | copy-start | bytes 50331652
  231.1 11.4 %copy-start.6 = (bf16[1,4096,192]{1,2,0:T(8,128)(2,1)S(1)}, bf16[1,4096,192]{1,2,0:T(8,128)(2,1)}, u32[]{:S(2)}) copy-start(bf16[1,4096,192]{1,2,0:T(8,128)(2,1)} %param.12) | copy-start | bytes 4718596
  269.0 3.0 copy-start.3
  269.0 3.1 copy-start.7
  272.1 23.1 %copy-start.4 = (bf16[1,1536,512]{2,1,0:T(8,128)(2,1)S(1)}, bf16[1,1536,512]{2,1,0:T(8,128)(2,1)}, u32[]{:S(2)}) copy-start(bf16[1,1536,512]{2,1,0:T(8,128)(2,1)} %param.13) | copy-start | bytes 4718596
  296.7 63.4 %all-to-all-start.4 = ((bf16[8,32,1,512]{3,0,2,1:T(8,128)(2,1)}), bf16[8,32,1,512]{3,0,2,1:T(8,128)(2,1)S(1)}, u32[]{:S(2)}, u32[]{:S(2)}) async-start(bf16[8,32,1,512]{3,0,2,1:T(8,128)(2,1)} %copy.58), calls=%async_computation.4 | async-start | bytes 524288 | tf_op jit(solution)/shard_map/all_to_all | solution.py:74
  360.1 35.8 %all-to-all-start.2 = ((bf16[8,32,8,512]{3,2,0,1:T(8,128)(2,1)}), bf16[8,32,8,512]{3,2,0,1:T(8,128)(2,1)}, u32[]{:S(2)}, u32[]{:S(2)}) async-start(bf16[8,32,8,512]{3,2,0,1:T(8,128)(2,1)} %copy.52), calls=%async_computation.2 | async-start | bytes 4194304 | tf_op jit(solution)/shard_map/all_to_all | solution.py:74
  398.1 2.3 copy-start.2
Sparse Core Ops, SparseCore 0:
  59.2 171.8 all-gather.5
  232.9 36.0 all-gather.9
  270.8 80.9 all-gather.7

commit v2 on v1

v2 whole, which is shorter than its diff:
```python
import jax
import jax.numpy as jnp
from jax import lax
from jax.sharding import PartitionSpec as P

MAIN = 8
FIRST_WIDTH = 1664


def per_device(tokens, router_weight, rollout_ids, source_row, gate_weight, up_weight, down_weight):
    owners = lax.axis_size("dp")
    columns = lax.axis_size("expert")
    tok_rows, model_width = tokens.shape
    top_count = rollout_ids.shape[1]
    hidden_part = gate_weight.shape[2]
    out_width = down_weight.shape[2]
    bf16, f32 = jnp.bfloat16, jnp.float32
    block_rows = columns * (MAIN + 1)
    slot_rows = owners * block_rows
    row_toks = columns * tok_rows
    first = FIRST_WIDTH
    second = model_width - first
    fold = -(-second // (MAIN * 128)) * 128

    raw = lax.all_gather(tokens[:, :first], "expert", axis=0, tiled=True)

    logits = jnp.dot(tokens.astype(f32), router_weight, precision=lax.Precision.HIGHEST)

    sent_ids = jnp.broadcast_to(rollout_ids.T[None], (owners, top_count, tok_rows))
    blocks = lax.all_to_all(sent_ids, "dp", split_axis=0, concat_axis=0, tiled=True)
    source_block = source_row[0] // (tok_rows * columns)
    block = lax.dynamic_index_in_dim(blocks, source_block, axis=0, keepdims=False)
    place = (source_row % tok_rows)[None, :] == jnp.arange(tok_rows, dtype=jnp.int32)[:, None]
    expert_ids = jnp.dot(
        block.astype(bf16), place.astype(bf16), preferred_element_type=f32
    ).astype(jnp.int32).T

    expert_iota = jnp.arange(router_weight.shape[1], dtype=jnp.int32)
    picks = jnp.any(expert_ids[:, :, None] == expert_iota[None, None, :], axis=1)
    chosen = picks[:, :owners]
    before = jnp.arange(tok_rows)[:, None] > jnp.arange(tok_rows)[None, :]
    slot_rank = jnp.dot(before.astype(bf16), chosen.astype(bf16), preferred_element_type=f32)
    slot_rank = jnp.where(chosen, slot_rank, -1.0)

    def select(lowest, count):
        slots = jnp.arange(lowest, lowest + count, dtype=f32)
        sel = slot_rank[:, :, None] == slots
        sel = sel.reshape(tok_rows, owners * count).astype(bf16)
        return lax.dot_general(
            sel, tokens[:, first:], (((0,), (0,)), ((), ())), preferred_element_type=f32
        ).astype(bf16)

    sent_main = select(0, MAIN).reshape(owners, MAIN, second)
    sent_last = jnp.pad(select(MAIN, 1), ((0, 0), (0, MAIN * fold - second)))
    sent_last = sent_last.reshape(owners, MAIN, fold)
    sent = jnp.concatenate([sent_main, sent_last], axis=2)
    arrived = lax.all_to_all(sent, "dp", split_axis=0, concat_axis=0, tiled=True)
    gathered = lax.all_gather(
        arrived.reshape(owners * MAIN, second + fold), "expert", axis=0, tiled=True
    )

    raised = jnp.where(picks, jnp.exp(jnp.where(picks, logits, 0.0)), 0.0)
    weights = raised / jnp.sum(raised, axis=1, keepdims=True)
    info = jnp.concatenate([slot_rank, weights[:, :owners]], axis=1).T
    infos = lax.all_to_all(
        jnp.broadcast_to(info[None], (columns,) + info.shape), "expert", 0, 0, tiled=True
    )
    infos = jnp.transpose(infos, (1, 0, 2)).reshape(2 * owners, 1, row_toks)
    row_rank, row_weight = infos[:owners], infos[owners:]

    row = jnp.arange(block_rows, dtype=jnp.int32)
    is_main = row < columns * MAIN
    row_column = jnp.where(is_main, row // MAIN, row - columns * MAIN)
    row_slot = jnp.where(is_main, row % MAIN, MAIN).astype(f32)
    tok_column = jnp.arange(row_toks, dtype=jnp.int32) // tok_rows
    same_column = row_column[:, None] == tok_column[None, :]
    taken = (row_rank == row_slot[None, :, None]) & same_column[None]

    first_sent = jnp.dot(
        taken.reshape(slot_rows, row_toks).astype(bf16), raw, preferred_element_type=f32
    ).astype(bf16)
    first_rows = lax.all_to_all(
        first_sent.reshape(owners, block_rows, first), "dp", split_axis=0, concat_axis=0, tiled=True
    ).reshape(slot_rows, first)

    both = jnp.concatenate([gate_weight[0], up_weight[0]], axis=1)
    first_val = jnp.dot(first_rows, both[:first], preferred_element_type=f32)
    first_val = first_val.reshape(owners, block_rows, 2 * hidden_part)

    wide = jnp.pad(both[first:], ((0, fold), (0, 0)))
    main_val = jnp.dot(gathered, wide, preferred_element_type=f32)
    main_val = main_val.reshape(columns, owners, MAIN, 2 * hidden_part)
    main_val = jnp.transpose(main_val, (1, 0, 2, 3)).reshape(owners, columns * MAIN, 2 * hidden_part)
    last_rows = gathered[:, second:].reshape(columns * owners, MAIN * fold)[:, :second]
    last_val = jnp.dot(last_rows, both[first:], preferred_element_type=f32)
    last_val = jnp.transpose(last_val.reshape(columns, owners, 2 * hidden_part), (1, 0, 2))
    value = first_val + jnp.concatenate([main_val, last_val], axis=1)
    value = value.reshape(slot_rows, 2 * hidden_part)
    hidden = (jax.nn.silu(value[:, :hidden_part]) * value[:, hidden_part:]).astype(bf16)

    full = lax.all_gather(hidden, "expert", axis=1, tiled=True)
    out = jnp.dot(full, down_weight[0], preferred_element_type=f32).astype(bf16)
    back = lax.all_to_all(
        out.reshape(owners, block_rows, out_width), "dp", split_axis=0, concat_axis=0, tiled=True
    ).reshape(slot_rows, out_width)

    mat = jnp.where(taken, row_weight, 0.0).reshape(slot_rows, row_toks)
    high = lax.reduce_precision(mat, 8, 7)
    low = (mat - high).astype(bf16)
    dims = (((0,), (0,)), ((), ()))
    part = lax.dot_general(high.astype(bf16), back, dims, preferred_element_type=f32)
    part = part + lax.dot_general(low, back, dims, preferred_element_type=f32)
    part = part.astype(bf16).reshape(columns, tok_rows, out_width)
    whole = lax.all_to_all(part, "expert", split_axis=0, concat_axis=0, tiled=True)
    return jnp.transpose(whole, (1, 0, 2)).reshape(tok_rows, model_width)


def solution(mesh):
    in_specs = (
        P(("dp", "expert"), None),
        P(),
        P(("dp", "expert"), None),
        P(("dp", "expert")),
        P("dp", None, "expert"),
        P("dp", None, "expert"),
        P("dp", None, "expert"),
    )
    out_specs = P(("dp", "expert"), None)
    return jax.shard_map(
        per_device, mesh=mesh, in_specs=in_specs, out_specs=out_specs, check_vma=False
    )
```

time: 442 us -> 404 us (0.914)
  blocking collectives: 119 us -> 56.2 us
  local copies, waits for them, and re-layouts: 13.9 us -> 29.7 us
  matrix products: 40.8 us -> 54.2 us
  waiting for transfers between devices: 216 us -> 208 us
  other arithmetic: 2.59 us -> 9.78 us
    all_gather x3, waiting for transfers between devices: 209 us -> 160 us  [the longest x1 82.5 us: per_device(): full = lax.all_gather(hidden, 'expert', axis=1, tiled=True)]
    all_gather x2 -> x0, blocking collectives: 43.6 us -> none  [the longest x1 22.3 us: expert(): full = lax.all_gather(hidden, 'expert', axis=0, tiled=True)]
    all_to_all x2 -> x3, waiting for transfers between devices: 3.23 us -> 43.3 us  [the longest x1 31.1 us: per_device(): lax.all_to_all(out.reshape(owners, block_rows, out_width), 'dp', split_ax...]
    all_to_all x2 -> x1, blocking collectives: 44.9 us -> 25.4 us  [per_device(): lax.all_to_all(sent, 'dp', split_axis=0, concat_axis=0, tiled=True)]
    dot_general x12 -> x9, matrix products: 38.7 us -> 52.2 us  [the longest x1 12.5 us: per_device(): jnp.dot(taken.reshape(slot_rows, row_toks).astype(bf16), raw, preferred_e...]
    unnamed x21 -> x18, local copies, waits for them, and re-layouts: 3.49 us -> 13.3 us
    slice x1 -> x3, local copies, waits for them, and re-layouts: 0.02 us -> 6.86 us  [the longest x1 2.7 us: per_device(): gathered[:, second:].reshape(columns * owners, MAIN * fold)[:, :second]]
    all_to_all x2 -> x3, starting transfers between devices: 24.4 us -> 20.8 us  [the longest x1 8.2 us: per_device(): lax.all_to_all(jnp.broadcast_to(info[None], (columns,) + info.shape), 'ex...]
  transfers between devices with their start and end apart: 6 -> 7, of which waited for: 5 -> 5; matrix products, arithmetic and copies ran while one was open for 10% -> 13% of each run, Pallas kernels for 0% -> 0%
where the time goes in v2:
time: 404 us; the launch traced here: 403 us
  waiting for transfers between devices  208 us (51%)
  blocking collectives  56.2 us (14%)
  matrix products  54.2 us (13%)
  local copies, waits for them, and re-layouts  29.7 us (7%)
  starting transfers between devices  29.7 us (7%)
  between operations  16 us (4%)
  other arithmetic  9.78 us (2%)
    all_gather x1, waiting for transfers between devices, per_device(): full = lax.all_gather(hidden, 'expert', axis=1, tiled=True)  82.5 us
    all_gather x1, waiting for transfers between devices, per_device(): lax.all_gather(arrived.reshape(owners * MAIN, second + fold), 'expert', a...  77.7 us
    all_to_all x1, waiting for transfers between devices, per_device(): lax.all_to_all(out.reshape(owners, block_rows, out_width), 'dp', split_ax...  31.1 us
    all_to_all x1, blocking collectives, per_device(): lax.all_to_all(part, 'expert', split_axis=0, concat_axis=0, tiled=True)  30.8 us
    all_to_all x1, blocking collectives, per_device(): lax.all_to_all(sent, 'dp', split_axis=0, concat_axis=0, tiled=True)  25.4 us
    unnamed x18, local copies, waits for them, and re-layouts  13.3 us
    dot_general x1, matrix products, per_device(): jnp.dot(taken.reshape(slot_rows, row_toks).astype(bf16), raw, preferred_e...  12.5 us
    all_to_all x1, waiting for transfers between devices, per_device(): lax.all_to_all(jnp.broadcast_to(info[None], (columns,) + info.shape), 'ex...  12.1 us
  transfers between devices with their start and end apart: 7, of which 5 were waited for; matrix products, arithmetic and copies ran while one was open for 13% of the time, Pallas kernels for 0%

profile of v2, /device:TPU:1, one launch (start us, length us, event | category | flops | bytes accessed | tf_op | source)
XLA Modules:
  0.0 403.5 jit_solution(5748705778154889135)
XLA Ops:
  6.5 0.0 copy-start
  6.5 0.0 copy-start.2
  6.5 0.0 all-gather.4.cloned.1.call-start
  6.5 1.9 slice.48
  8.5 0.0 all-gather.4.cloned.1.call-update
  8.5 1.3 broadcast_in_dim.25
  9.9 8.6 %all-to-all-start = ((s32[32,8,128]{2,1,0:T(8,128)}), s32[32,8,128]{2,1,0:T(8,128)S(1)}, u32[]{:S(2)}, u32[]{:S(2)}) async-start(s32[32,8,128]{2,1,0:T(8,128)} %broadcast_in_dim.25), calls=%async_computation | async-start | bytes 262144 | tf_op jit(solution)/shard_map/all_to_all | solution.py:30
  18.5 0.0 all-gather.6.cloned.1.call-start
  21.1 0.1 eq.133
  21.2 0.7 and_select_fusion.2
  21.9 4.3 %all-to-all-done = s32[32,8,128]{2,1,0:T(8,128)S(1)} async-done(((s32[32,8,128]{2,1,0:T(8,128)}), s32[32,8,128]{2,1,0:T(8,128)S(1)}, u32[]{:S(2)}, u32[]{:S(2)}) %all-to-all-start) | async-done | bytes 131104 | tf_op jit(solution)/shard_map/all_to_all | solution.py:30
  26.2 0.1 convolution_convert_fusion.4
  26.3 0.1 copy.38
  26.4 0.3 fusion.28
  26.7 0.1 copy.39
  26.8 0.1 convolution_select_fusion.1
  26.9 1.3 convolution_convert_fusion.3
  28.3 0.0 copy-done.2
  28.3 0.5 fusion.15
  28.8 0.1 pad_maximum_fusion.1
  28.9 25.4 %all_to_all.30 = bf16[32,8,2816]{2,1,0:T(8,128)(2,1)} all-to-all(bf16[32,8,2816]{2,1,0:T(8,128)(2,1)S(1)} %pad_maximum_fusion.1), channel_id=1, replica_groups=mesh['dp'=32,'expert'=8] {'dp'}, dimensions={0} | all-to-all | bytes 2883584 | tf_op jit(solution)/shard_map/all_to_all | solution.py:57
  54.3 0.0 all-gather.6.cloned.1.call-update
  54.3 0.0 copy-done
  54.4 1.8 fusion.49
  56.2 0.7 broadcast_in_dim.28
  56.9 8.2 %all-to-all-start.1 = ((f32[8,64,128]{2,1,0:T(8,128)}), f32[8,64,128]{2,1,0:T(8,128)S(1)}, u32[]{:S(2)}, u32[]{:S(2)}) async-start(f32[8,64,128]{2,1,0:T(8,128)} %broadcast_in_dim.28), calls=%async_computation.1 | async-start | bytes 524288 | tf_op jit(solution)/shard_map/all_to_all | solution.py:65
  65.1 0.1 eq.127
  65.2 0.1 broadcast_compare_fusion
  65.4 12.1 %all-to-all-done.1 = f32[8,64,128]{2,1,0:T(8,128)S(1)} async-done(((f32[8,64,128]{2,1,0:T(8,128)}), f32[8,64,128]{2,1,0:T(8,128)S(1)}, u32[]{:S(2)}, u32[]{:S(2)}) %all-to-all-start.1) | async-done | bytes 262176 | tf_op jit(solution)/shard_map/all_to_all | solution.py:65
  77.5 1.8 fusion.1
  79.3 0.0 all-gather.4.cloned.1.call-done
  79.3 12.5 %convolution_convert_fusion = bf16[2304,1664]{1,0:T(8,128)(2,1)} fusion(pred[2304,1024]{1,0:T(32,128)(4,1)S(1)} %fusion.1, bf16[1024,1664]{1,0:T(8,128)(2,1)} %all-gather.4.cloned.1.call-done), kind=kOutput, calls=%fused_computation.2 | convolution fusion | flops 7855570944 | bytes 13434880 | tf_op jit(solution)/shard_map/dot_general | solution.py:79
  91.9 5.1 %all-to-all-start.2 = ((bf16[32,72,1664]{2,1,0:T(8,128)(2,1)}), bf16[32,72,1664]{2,1,0:T(8,128)(2,1)}, u32[]{:S(2)}, u32[]{:S(2)}) async-start(bf16[32,72,1664]{2,1,0:T(8,128)(2,1)} %bitcast.78), calls=%async_computation.2 | async-start | bytes 15335424 | tf_op jit(solution)/shard_map/all_to_all | solution.py:82
  97.0 0.2 all-gather.8.cloned.1.call-start
  97.2 3.2 copy.45
  100.4 3.9 copy.44
  104.3 3.3 pad_maximum_fusion
  107.6 77.7 %all-gather.6.cloned.1.call-done = bf16[2048,2816]{1,0:T(8,128)(2,1)} async-done(((bf16[256,2816]{1,0:T(8,128)(2,1)}), bf16[2048,2816]{1,0:T(8,128)(2,1)}) %all-gather.6.cloned.1.call-update) | async-done | bytes 11534352 | tf_op jit(solution)/shard_map/all_gather | solution.py:58
  185.3 2.7 slice.60
  188.0 3.7 reshape.157
  191.7 2.8 fusion.22
  194.5 0.2 copy.62
  194.8 0.0 copy-done.4
  194.8 8.9 %fusion.16 = f32[2048,384]{1,0:T(8,128)S(1)} fusion(bf16[2048,2816]{1,0:T(8,128)(2,1)} %all-gather.6.cloned.1.call-done, bf16[2432,384]{1,0:T(8,128)(2,1)S(1)} %copy-done.4), kind=kOutput, calls=%fused_computation.25 | convolution fusion | flops 4429185024 | bytes 16547840 | tf_op jit(solution)/shard_map/dot_general | solution.py:91
  203.7 2.0 copy.61
  205.8 0.0 all-to-all-done.2
  205.8 9.1 %maximum_add_fusion = f32[32,72,384]{2,1,0:T(8,128)S(1)} fusion(f32[32,8,384]{2,1,0:T(8,128)S(1)} %bitcast.92, f32[32,64,384]{2,1,0:T(8,128)} %bitcast.82, bf16[32,72,1664]{2,1,0:T(8,128)(2,1)} %all-to-all-done.2, bf16[4096,192]{1,0:T(8,128)(2,1)S(1)} %bitcast.75, bf16[4096,192]{1,0:T(8,128)(2,1)} %bitcast.77), kind=kOutput, calls=%fused_computation.22 | convolution fusion | flops 2948726784 | bytes 17891328 | tf_op jit(solution)/shard_map/dot_general | solution.py:87
  214.9 2.2 fusion.48
  217.1 3.0 copy.52
  220.1 1.8 copy.51
  221.9 3.5 multiply_convert_fusion
  225.5 0.0 all-gather.8.cloned.1.call-update
  225.5 82.5 %all-gather.8.cloned.1.call-done = bf16[2304,1536]{0,1:T(8,128)(2,1)} async-done(((bf16[2304,192]{0,1:T(8,128)(2,1)}), bf16[2304,1536]{0,1:T(8,128)(2,1)}) %all-gather.8.cloned.1.call-update) | async-done | bytes 7077904 | tf_op jit(solution)/shard_map/all_gather | solution.py:101
  308.0 0.0 copy-done.5
  308.0 8.2 %convolution_convert_fusion.1 = bf16[2304,512]{1,0:T(8,128)(2,1)} fusion(bf16[2304,1536]{0,1:T(8,128)(2,1)} %all-gather.8.cloned.1.call-done, bf16[1,1536,512]{2,1,0:T(8,128)(2,1)S(1)} %copy-done.5), kind=kOutput, calls=%fused_computation.19 | convolution fusion | flops 3625058304 | bytes 11010048 | tf_op jit(solution)/shard_map/dot_general | solution.py:102
  316.3 7.5 %all-to-all-start.4 = ((bf16[32,72,512]{2,1,0:T(8,128)(2,1)}), bf16[32,72,512]{2,1,0:T(8,128)(2,1)S(1)}, u32[]{:S(2)}, u32[]{:S(2)}) async-start(bf16[32,72,512]{2,1,0:T(8,128)(2,1)} %bitcast.84), calls=%async_computation.4 | async-start | bytes 4718592 | tf_op jit(solution)/shard_map/all_to_all | solution.py:103
  323.8 31.1 %all-to-all-done.4 = bf16[32,72,512]{2,1,0:T(8,128)(2,1)S(1)} async-done(((bf16[32,72,512]{2,1,0:T(8,128)(2,1)}), bf16[32,72,512]{2,1,0:T(8,128)(2,1)S(1)}, u32[]{:S(2)}, u32[]{:S(2)}) %all-to-all-start.4) | async-done | bytes 2359328 | tf_op jit(solution)/shard_map/all_to_all | solution.py:103
  354.9 1.4 copy-done.3
  356.3 3.7 fusion.2
  360.1 0.0 copy-start.1
  360.1 5.0 %fusion.18 = bf16[1024,512]{1,0:T(8,128)(2,1)S(1)} fusion(f32[1024,512,1]{1,0,2:T(8,128)S(1)} %fusion.2, bf16[32,72,512]{2,1,0:T(8,128)(2,1)} %copy-done.3, f32[32,1024]{1,0:T(8,128)S(1)} %bitcast.95, f32[32,1024]{1,0:T(8,128)S(1)} %bitcast.91, f32[72]{0:T(128)S(1)} %fusion.40, pred[72,1024]{1,0:T(8,128)(4,1)S(1)} %broadcast_compare_fusion), kind=kOutput, calls=%fused_computation.28 | convolution fusion | flops 2428764160 | bytes 5841184 | tf_op jit(solution)/shard_map/dot_general | solution.py:111
  365.1 30.8 %all_to_all.31 = bf16[8,128,512]{2,1,0:T(8,128)(2,1)S(1)} all-to-all(bf16[8,128,512]{2,1,0:T(8,128)(2,1)S(1)} %bitcast.85), channel_id=1, replica_groups=mesh['dp'=32,'expert'=8] {'expert'}, dimensions={0} | all-to-all | bytes 2097152 | tf_op jit(solution)/shard_map/all_to_all | solution.py:114
  395.9 1.1 copy.55
  396.9 0.0 copy-done.1
  (15 shorter events, 0.1 us)
Async XLA Ops:
  6.5 47.8 %copy-start = (f32[4096,128]{1,0:T(8,128)S(1)}, f32[4096,128]{1,0:T(8,128)}, u32[]{:S(2)}) copy-start(f32[4096,128]{1,0:T(8,128)} %param.8) | copy-start | bytes 6291460
  6.5 21.7 %copy-start.2 = (bf16[128,4096]{1,0:T(8,128)(2,1)S(1)}, bf16[128,4096]{1,0:T(8,128)(2,1)}, u32[]{:S(2)}) copy-start(bf16[128,4096]{1,0:T(8,128)(2,1)} %param.7) | copy-start | bytes 3145732
  6.5 72.8 %all-gather.4.cloned.1.call-start = ((), (), s32[]{:S(2)}) async-start(), calls=%async_computation.6 | async-start | bytes 3833856 | tf_op jit(solution)/shard_map/all_gather | solution.py:25
  9.9 16.3 %all-to-all-start = ((s32[32,8,128]{2,1,0:T(8,128)}), s32[32,8,128]{2,1,0:T(8,128)S(1)}, u32[]{:S(2)}, u32[]{:S(2)}) async-start(s32[32,8,128]{2,1,0:T(8,128)} %broadcast_in_dim.25), calls=%async_computation | async-start | bytes 262144 | tf_op jit(solution)/shard_map/all_to_all | solution.py:30
  18.5 166.8 %all-gather.6.cloned.1.call-start = ((), (), s32[]{:S(2)}) async-start(), calls=%async_computation.7 | async-start | bytes 12976128 | tf_op jit(solution)/shard_map/all_gather | solution.py:58
  56.9 20.6 %all-to-all-start.1 = ((f32[8,64,128]{2,1,0:T(8,128)}), f32[8,64,128]{2,1,0:T(8,128)S(1)}, u32[]{:S(2)}, u32[]{:S(2)}) async-start(f32[8,64,128]{2,1,0:T(8,128)} %broadcast_in_dim.28), calls=%async_computation.1 | async-start | bytes 524288 | tf_op jit(solution)/shard_map/all_to_all | solution.py:65
  91.9 113.9 %all-to-all-start.2 = ((bf16[32,72,1664]{2,1,0:T(8,128)(2,1)}), bf16[32,72,1664]{2,1,0:T(8,128)(2,1)}, u32[]{:S(2)}, u32[]{:S(2)}) async-start(bf16[32,72,1664]{2,1,0:T(8,128)(2,1)} %bitcast.78), calls=%async_computation.2 | async-start | bytes 15335424 | tf_op jit(solution)/shard_map/all_to_all | solution.py:82
  97.0 211.1 %all-gather.8.cloned.1.call-start = ((), (), s32[]{:S(2)}) async-start(), calls=%async_computation.8 | async-start | bytes 7962624 | tf_op jit(solution)/shard_map/all_gather | solution.py:101
  191.7 3.1 copy-start.4
  221.9 86.1 %copy-start.5 = (bf16[1,1536,512]{2,1,0:T(8,128)(2,1)S(1)}, bf16[1,1536,512]{2,1,0:T(8,128)(2,1)}, u32[]{:S(2)}) copy-start(bf16[1,1536,512]{2,1,0:T(8,128)(2,1)} %param.13) | copy-start | bytes 4718596
  316.3 38.7 %all-to-all-start.4 = ((bf16[32,72,512]{2,1,0:T(8,128)(2,1)}), bf16[32,72,512]{2,1,0:T(8,128)(2,1)S(1)}, u32[]{:S(2)}, u32[]{:S(2)}) async-start(bf16[32,72,512]{2,1,0:T(8,128)(2,1)} %bitcast.84), calls=%async_computation.4 | async-start | bytes 4718592 | tf_op jit(solution)/shard_map/all_to_all | solution.py:103
  354.9 1.4 copy-start.3
  360.1 36.8 %copy-start.1 = (f32[4096,128]{1,0:T(8,128)S(1)}, f32[4096,128]{1,0:T(8,128)}, u32[]{:S(2)}) copy-start(f32[4096,128]{1,0:T(8,128)} %param.8) | copy-start | bytes 6291460
Sparse Core Ops, SparseCore 0:
  9.1 51.2 all-gather.3
  62.2 123.0 all-gather.5
  225.6 82.3 all-gather.7

commit v3 on v2

v3 whole, which is shorter than its diff:
```python
import functools

import jax
import jax.numpy as jnp
from jax import lax
from jax.experimental import pallas as pl
from jax.experimental.pallas import tpu as pltpu
from jax.sharding import PartitionSpec as P

MAIN = 8
FIRST_WIDTH = 1792
STEP = 256
VMEM_BYTES = 48 * 1024 * 1024
bf16, f32 = jnp.bfloat16, jnp.float32


def iota(shape, dim):
    return lax.broadcasted_iota(jnp.int32, shape, dim)


def first_dispatch_kernel(columns, tok_rows, rank_ref, raw_ref, out_ref, pair_sel, last_sel):
    owners = rank_ref.shape[0]
    pairs = columns // 2
    pair_toks, pair_rows = 2 * tok_rows, 2 * MAIN

    @pl.when(pl.program_id(0) == 0)
    def _():
        row, tok = iota((pair_rows, pair_toks), 0), iota((pair_rows, pair_toks), 1)
        wanted = jnp.where(row // MAIN == tok // tok_rows, row % MAIN, -2).astype(f32)
        for pair in range(pairs):
            rank = rank_ref[:, :, pair * pair_toks : (pair + 1) * pair_toks]
            sel = jnp.where(rank == wanted[None], 1.0, 0.0).astype(bf16)
            pair_sel[pair] = sel.reshape(owners * pair_rows, pair_toks)
        row, tok = iota((columns, columns * tok_rows), 0), iota((columns, columns * tok_rows), 1)
        wanted = jnp.where(row == tok // tok_rows, MAIN, -2).astype(f32)
        sel = jnp.where(rank_ref[...] == wanted[None], 1.0, 0.0)
        last_sel[...] = sel.reshape(owners * columns, columns * tok_rows).astype(bf16)

    for pair in range(pairs):
        rows = jnp.dot(
            pair_sel[pair],
            raw_ref[pair * pair_toks : (pair + 1) * pair_toks, :],
            preferred_element_type=f32,
        ).astype(bf16)
        out_ref[:, pair * pair_rows : (pair + 1) * pair_rows, :] = rows.reshape(
            owners, pair_rows, rows.shape[1]
        )
    rows = jnp.dot(last_sel[...], raw_ref[...], preferred_element_type=f32)
    out_ref[:, columns * MAIN :, :] = rows.reshape(owners, columns, rows.shape[1]).astype(bf16)


def first_dispatch(rank, raw, columns, tok_rows):
    owners = rank.shape[0]
    row_toks, width = raw.shape
    block_rows = columns * (MAIN + 1)
    pairs = columns // 2
    return pl.pallas_call(
        functools.partial(first_dispatch_kernel, columns, tok_rows),
        grid=(width // STEP,),
        in_specs=[
            pl.BlockSpec((owners, 1, row_toks), lambda f: (0, 0, 0)),
            pl.BlockSpec((row_toks, STEP), lambda f: (0, f)),
        ],
        out_specs=pl.BlockSpec((owners, block_rows, STEP), lambda f: (0, 0, f)),
        out_shape=jax.ShapeDtypeStruct((owners, block_rows, width), bf16),
        scratch_shapes=[
            pltpu.VMEM((pairs, owners * 2 * MAIN, 2 * tok_rows), bf16),
            pltpu.VMEM((owners * columns, row_toks), bf16),
        ],
        compiler_params=pltpu.CompilerParams(vmem_limit_bytes=VMEM_BYTES),
    )(rank, raw)


def hidden_kernel(main_steps, x_ref, w_ref, v_ref, o_ref):
    columns, rows, width = x_ref.shape
    half = w_ref.shape[1] // 2
    acc = jnp.dot(x_ref[...].reshape(columns * rows, width), w_ref[...], preferred_element_type=f32)

    def finish(acc):
        val = acc + v_ref[...]
        gate, up = val[:, :half], val[:, half:]
        hidden = gate / (1.0 + jnp.exp(-gate)) * up
        o_ref[...] = hidden.T[: o_ref.shape[0]].astype(bf16)

    @pl.when(pl.program_id(0) < main_steps)
    def _():
        pieces = [
            acc[(j * rows + i) : (j * rows + i + MAIN)]
            for i in range(0, rows, MAIN)
            for j in range(columns)
        ]
        finish(jnp.concatenate(pieces, axis=0))

    @pl.when(pl.program_id(0) == main_steps)
    def _():
        finish(acc)


def hidden_rows(gathered, weight, first_val, hidden_part):
    columns, col_rows, width = gathered.shape
    steps = MAIN + 1
    rows = col_rows // steps
    step_rows = columns * rows
    return pl.pallas_call(
        functools.partial(hidden_kernel, MAIN),
        grid=(steps,),
        in_specs=[
            pl.BlockSpec((columns, rows, width), lambda b: (0, b, 0)),
            pl.BlockSpec(weight.shape, lambda b: (0, 0)),
            pl.BlockSpec((step_rows, weight.shape[1]), lambda b: (b, 0)),
        ],
        out_specs=pl.BlockSpec((hidden_part, step_rows), lambda b: (0, b)),
        out_shape=jax.ShapeDtypeStruct((hidden_part, steps * step_rows), bf16),
        compiler_params=pltpu.CompilerParams(vmem_limit_bytes=VMEM_BYTES),
    )(gathered, weight, first_val)


def per_device(tokens, router_weight, rollout_ids, source_row, gate_weight, up_weight, down_weight):
    owners = lax.axis_size("dp")
    columns = lax.axis_size("expert")
    tok_rows, model_width = tokens.shape
    top_count = rollout_ids.shape[1]
    hidden_part = gate_weight.shape[2]
    out_width = down_weight.shape[2]
    block_rows = columns * (MAIN + 1)
    slot_rows = owners * block_rows
    row_toks = columns * tok_rows
    first = FIRST_WIDTH
    second = model_width - first
    fold = -(-second // (MAIN * 128)) * 128
    main_rows = owners * columns * MAIN

    raw = lax.all_gather(tokens[:, :first], "expert", axis=0, tiled=True)

    logits = jnp.dot(tokens.astype(f32), router_weight, precision=lax.Precision.HIGHEST)

    sent_ids = jnp.broadcast_to(rollout_ids.T[None], (owners, top_count, tok_rows))
    blocks = lax.all_to_all(sent_ids, "dp", split_axis=0, concat_axis=0, tiled=True)
    source_block = source_row[0] // (tok_rows * columns)
    block = lax.dynamic_index_in_dim(blocks, source_block, axis=0, keepdims=False)
    place = (source_row % tok_rows)[None, :] == jnp.arange(tok_rows, dtype=jnp.int32)[:, None]
    expert_ids = jnp.dot(
        block.astype(bf16), place.astype(bf16), preferred_element_type=f32
    ).astype(jnp.int32).T

    expert_iota = jnp.arange(router_weight.shape[1], dtype=jnp.int32)
    picks = jnp.any(expert_ids[:, :, None] == expert_iota[None, None, :], axis=1)
    chosen = picks[:, :owners]
    before = jnp.arange(tok_rows)[:, None] > jnp.arange(tok_rows)[None, :]
    slot_rank = jnp.dot(before.astype(bf16), chosen.astype(bf16), preferred_element_type=f32)
    slot_rank = jnp.where(chosen, slot_rank, -1.0)

    def whole_row(info):
        sent = jnp.broadcast_to(info.T[None], (columns, owners, tok_rows))
        got = lax.all_to_all(sent, "expert", split_axis=0, concat_axis=0, tiled=True)
        return jnp.transpose(got, (1, 0, 2)).reshape(owners, 1, row_toks)

    row_rank = whole_row(slot_rank.astype(bf16)).astype(f32)

    def select(lowest, count):
        slots = jnp.arange(lowest, lowest + count, dtype=f32)
        sel = slot_rank[:, :, None] == slots
        sel = sel.reshape(tok_rows, owners * count).astype(bf16)
        return lax.dot_general(
            sel, tokens[:, first:], (((0,), (0,)), ((), ())), preferred_element_type=f32
        ).astype(bf16)

    sent_main = select(0, MAIN).reshape(owners, MAIN, second)
    sent_last = jnp.pad(select(MAIN, 1), ((0, 0), (0, MAIN * fold - second)))
    sent_last = sent_last.reshape(owners, MAIN, fold)
    sent = jnp.concatenate([sent_main, sent_last], axis=2)
    arrived = lax.all_to_all(sent, "dp", split_axis=0, concat_axis=0, tiled=True)
    arrived_main = arrived[:, :, :second].reshape(owners * MAIN, second)
    arrived_last = arrived[:, :, second:].reshape(owners, MAIN * fold)[:, :second]
    gathered = lax.all_gather(
        jnp.concatenate([arrived_main, arrived_last], axis=0), "expert", axis=0
    )

    first_sent = first_dispatch(row_rank, raw, columns, tok_rows)
    first_rows = lax.all_to_all(first_sent, "dp", split_axis=0, concat_axis=0, tiled=True)

    half = -(-hidden_part // 128) * 128
    pad = ((0, 0), (0, half - hidden_part))
    both = jnp.concatenate([jnp.pad(gate_weight[0], pad), jnp.pad(up_weight[0], pad)], axis=1)
    first_val = jnp.dot(
        first_rows.reshape(slot_rows, first), both[:first], preferred_element_type=f32
    ).reshape(owners, block_rows, 2 * half)
    first_main = first_val[:, : columns * MAIN].reshape(main_rows, 2 * half)
    first_last = jnp.transpose(first_val[:, columns * MAIN :], (1, 0, 2))
    first_val = jnp.concatenate([first_main, first_last.reshape(-1, 2 * half)], axis=0)

    hidden = hidden_rows(gathered, both[first:], first_val, hidden_part)
    full = lax.all_gather(hidden, "expert", axis=0, tiled=True)
    out = lax.dot_general(
        full, down_weight[0], (((0,), (0,)), ((), ())), preferred_element_type=f32
    ).astype(bf16)
    out_main = out[:main_rows].reshape(owners, columns * MAIN, out_width)
    out_last = jnp.transpose(out[main_rows:].reshape(columns, owners, out_width), (1, 0, 2))
    out = jnp.concatenate([out_main, out_last], axis=1)
    back = lax.all_to_all(out, "dp", split_axis=0, concat_axis=0, tiled=True)
    back = back.reshape(slot_rows, out_width)

    raised = jnp.where(picks, jnp.exp(jnp.where(picks, logits, 0.0)), 0.0)
    weights = raised / jnp.sum(raised, axis=1, keepdims=True)
    row_weight = whole_row(weights[:, :owners])
    row = jnp.arange(block_rows, dtype=jnp.int32)
    is_main = row < columns * MAIN
    row_column = jnp.where(is_main, row // MAIN, row - columns * MAIN)
    row_slot = jnp.where(is_main, row % MAIN, MAIN).astype(f32)
    tok_column = jnp.arange(row_toks, dtype=jnp.int32) // tok_rows
    same_column = row_column[:, None] == tok_column[None, :]
    taken = (row_rank == row_slot[None, :, None]) & same_column[None]
    mat = jnp.where(taken, row_weight, 0.0).reshape(slot_rows, row_toks)
    high = lax.reduce_precision(mat, 8, 7)
    low = (mat - high).astype(bf16)
    dims = (((0,), (0,)), ((), ()))
    part = lax.dot_general(high.astype(bf16), back, dims, preferred_element_type=f32)
    part = part + lax.dot_general(low, back, dims, preferred_element_type=f32)
    part = part.astype(bf16).reshape(columns, tok_rows, out_width)
    whole = lax.all_to_all(part, "expert", split_axis=0, concat_axis=0, tiled=True)
    return jnp.transpose(whole, (1, 0, 2)).reshape(tok_rows, model_width)


def solution(mesh):
    in_specs = (
        P(("dp", "expert"), None),
        P(),
        P(("dp", "expert"), None),
        P(("dp", "expert")),
        P("dp", None, "expert"),
        P("dp", None, "expert"),
        P("dp", None, "expert"),
    )
    out_specs = P(("dp", "expert"), None)
    return jax.shard_map(
        per_device, mesh=mesh, in_specs=in_specs, out_specs=out_specs, check_vma=False
    )
```

time: 404 us -> 411 us (1.017)
  matrix products: 54.2 us -> 28.8 us
  Pallas kernels: 0 us -> 19.7 us
  blocking collectives: 56.2 us -> 70.5 us
  waiting for transfers between devices: 208 us -> 217 us
  local copies, waits for them, and re-layouts: 29.7 us -> 21.8 us
    all_to_all x3, waiting for transfers between devices: 43.3 us -> 120 us  [the longest x1 89.4 us: per_device(): lax.all_to_all(first_sent, 'dp', split_axis=0, concat_axis=0, tiled=True)]
    all_gather x2, waiting for transfers between devices: 160 us -> 92 us  [the longest x1 92 us: per_device(): full = lax.all_gather(hidden, 'expert', axis=0, tiled=True)]
    dot_general x5 -> x2, matrix products: 41.6 us -> 14.7 us  [the longest x1 7.43 us: per_device(): jnp.dot(first_rows.reshape(slot_rows, first), both[:first], preferred_ele...]
    pallas_call x0 -> x2, Pallas kernels: none -> 19.7 us  [the longest x1 12.6 us: hidden_rows(): pl.pallas_call(functools.partial(hidden_kernel, MAIN), grid=(steps,), in_...]
    all_to_all x0 -> x1, blocking collectives: none -> 15.1 us  [whole_row(): lax.all_to_all(sent, 'expert', split_axis=0, concat_axis=0, tiled=True)]
    reshape x3 -> x2, local copies, waits for them, and re-layouts: 5.97 us -> 0.23 us  [the longest x1 0.15 us: per_device(): out[main_rows:].reshape(columns, owners, out_width)]
    concatenate x1 -> x4, other arithmetic: 3.32 us -> 8.11 us  [the longest x1 2.72 us: per_device(): jnp.concatenate([first_main, first_last.reshape(-1, 2 * half)], axis=0)]
    unnamed x18 -> x14, local copies, waits for them, and re-layouts: 13.3 us -> 13.5 us
  transfers between devices with their start and end apart: 7 -> 7, of which waited for: 5 -> 4; matrix products, arithmetic and copies ran while one was open for 13% -> 10% of each run, Pallas kernels for 0% -> 2%
where the time goes in v3:
time: 411 us; the launch traced here: 410 us
  waiting for transfers between devices  217 us (53%)
  blocking collectives  70.5 us (17%)
  matrix products  28.8 us (7%)
  starting transfers between devices  27 us (7%)
  local copies, waits for them, and re-layouts  21.8 us (5%)
  Pallas kernels  19.7 us (5%)
  between operations  16 us (4%)
  other arithmetic  9.29 us (2%)
    all_gather x1, waiting for transfers between devices, per_device(): full = lax.all_gather(hidden, 'expert', axis=0, tiled=True)  92 us
    all_to_all x1, waiting for transfers between devices, per_device(): lax.all_to_all(first_sent, 'dp', split_axis=0, concat_axis=0, tiled=True)  89.4 us
    all_to_all x1, waiting for transfers between devices, per_device(): back = lax.all_to_all(out, 'dp', split_axis=0, concat_axis=0, tiled=True)  31 us
    all_to_all x1, blocking collectives, per_device(): lax.all_to_all(part, 'expert', split_axis=0, concat_axis=0, tiled=True)  30.9 us
    all_to_all x1, blocking collectives, per_device(): lax.all_to_all(sent, 'dp', split_axis=0, concat_axis=0, tiled=True)  24.5 us
    all_to_all x1, blocking collectives, whole_row(): lax.all_to_all(sent, 'expert', split_axis=0, concat_axis=0, tiled=True)  15.1 us
    unnamed x14, local copies, waits for them, and re-layouts  13.5 us
    pallas_call x1, Pallas kernels, hidden_rows(): pl.pallas_call(functools.partial(hidden_kernel, MAIN), grid=(steps,), in_...  12.6 us
  transfers between devices with their start and end apart: 7, of which 4 were waited for; matrix products, arithmetic and copies ran while one was open for 10% of the time, Pallas kernels for 2%

profile of v3, /device:TPU:1, one launch (start us, length us, event | category | flops | bytes accessed | tf_op | source)
XLA Modules:
  0.0 409.9 jit_solution(4262408467011669281)
XLA Ops:
  6.5 0.0 copy-start
  6.5 0.0 copy-start.4
  6.5 0.0 all-gather.5.cloned.1.call-start
  6.5 2.0 slice.51
  8.5 0.0 all-gather.5.cloned.1.call-update
  8.5 1.4 broadcast_in_dim.26
  9.9 8.6 %all-to-all-start = ((s32[32,8,128]{2,1,0:T(8,128)}), s32[32,8,128]{2,1,0:T(8,128)S(1)}, u32[]{:S(2)}, u32[]{:S(2)}) async-start(s32[32,8,128]{2,1,0:T(8,128)} %broadcast_in_dim.26), calls=%async_computation | async-start | bytes 262144 | tf_op jit(solution)/shard_map/all_to_all | solution.py:138
  18.5 0.0 all-gather.9.cloned.1.call-start
  21.2 0.1 eq.108
  21.3 0.7 and_select_fusion.2
  21.9 4.3 %all-to-all-done = s32[32,8,128]{2,1,0:T(8,128)S(1)} async-done(((s32[32,8,128]{2,1,0:T(8,128)}), s32[32,8,128]{2,1,0:T(8,128)S(1)}, u32[]{:S(2)}, u32[]{:S(2)}) %all-to-all-start) | async-done | bytes 131104 | tf_op jit(solution)/shard_map/all_to_all | solution.py:138
  26.2 0.1 convolution_convert_fusion.3
  26.3 0.1 copy.37
  26.4 0.3 fusion.23
  26.7 0.1 copy.38
  26.8 0.1 convolution_select_fusion.1
  27.0 1.3 convolution_convert_fusion.2
  28.3 0.0 copy-done.4
  28.3 0.5 fusion.17
  28.8 0.1 pad_maximum_fusion.2
  28.9 24.5 %all_to_all.35 = bf16[32,8,2688]{2,1,0:T(8,128)(2,1)S(1)} all-to-all(bf16[32,8,2688]{2,1,0:T(8,128)(2,1)S(1)} %pad_maximum_fusion.2), channel_id=1, replica_groups=mesh['dp'=32,'expert'=8] {'dp'}, dimensions={0} | all-to-all | bytes 2752512 | tf_op jit(solution)/shard_map/all_to_all | solution.py:172
  53.5 0.1 slice_bitcast_fusion.2
  53.6 1.2 pad_maximum_fusion.3
  54.8 0.0 all-gather.9.cloned.1.call-update
  54.8 15.1 %all_to_all.36 = bf16[8,32,128]{2,1,0:T(8,128)(2,1)S(1)} all-to-all(bf16[8,32,128]{2,1,0:T(8,128)(2,1)S(1)} %broadcast_in_dim.29), channel_id=1, replica_groups=mesh['dp'=32,'expert'=8] {'expert'}, dimensions={0} | all-to-all | bytes 131072 | tf_op jit(solution)/shard_map/all_to_all | solution.py:155
  69.9 0.1 copy.39
  70.0 0.0 all-gather.5.cloned.1.call-done.raw_ref
  70.0 0.0 copy-start.2
  70.1 2.0 copy-done.2
  72.1 7.1 %shard_map.73 = bf16[32,72,1792]{2,1,0:T(8,128)(2,1)} custom-call(f32[32,1,1024]{2,1,0:T(1,128)S(1)} %bitcast.69, bf16[1024,1792]{1,0:T(8,128)(2,1)S(1)} %copy-done.2), custom_call_target="tpu_custom_call" | custom-call | tf_op jit(solution)/shard_map/pallas_call | solution.py:57
  79.1 6.1 %all-to-all-start.4 = ((bf16[32,72,1792]{2,1,0:T(8,128)(2,1)}), bf16[32,72,1792]{2,1,0:T(8,128)(2,1)}, u32[]{:S(2)}, u32[]{:S(2)}) async-start(bf16[32,72,1792]{2,1,0:T(8,128)(2,1)} %shard_map.73), calls=%async_computation.4 | async-start | bytes 16515072 | tf_op jit(solution)/shard_map/all_to_all | solution.py:180
  85.2 0.0 all-gather.7.cloned.1.call-start
  85.3 3.8 copy.43
  89.1 3.9 copy.44
  93.0 2.6 fusion.16
  95.6 0.0 copy-start.3
  95.6 2.1 copy-done.3
  97.7 1.6 slice.62.w_ref
  99.3 89.4 %all-to-all-done.4 = bf16[32,72,1792]{2,1,0:T(8,128)(2,1)} async-done(((bf16[32,72,1792]{2,1,0:T(8,128)(2,1)}), bf16[32,72,1792]{2,1,0:T(8,128)(2,1)}, u32[]{:S(2)}, u32[]{:S(2)}) %all-to-all-start.4) | async-done | bytes 8257568 | tf_op jit(solution)/shard_map/all_to_all | solution.py:180
  188.7 7.4 %fusion.19 = f32[32,72,512]{2,1,0:T(8,128)S(1)} fusion(bf16[32,72,1792]{2,1,0:T(8,128)(2,1)} %all-to-all-done.4, bf16[4096,512]{1,0:T(8,128)(2,1)} %copy-done.3), kind=kOutput, calls=%fused_computation.30 | convolution fusion | flops 4227858432 | bytes 14811136 | tf_op jit(solution)/shard_map/dot_general | solution.py:185
  196.1 0.5 slice.64
  196.6 0.3 copy.46
  197.0 2.7 pad_maximum_fusion.v_ref
  199.7 0.0 all-gather.9.cloned.1.call-done
  199.7 1.7 copy-done.1
  201.3 12.6 %shard_map.74 = bf16[192,2304]{1,0:T(8,128)(2,1)} custom-call(bf16[8,288,2304]{2,1,0:T(8,128)(2,1)} %bitcast.71, bf16[2304,512]{1,0:T(8,128)(2,1)S(1)} %copy-done.1, f32[2304,512]{1,0:T(8,128)} %pad_maximum_fusion.v_ref), custom_call_target="tpu_custom_call" | custom-call | tf_op jit(solution)/shard_map/pallas_call | solution.py:104
  214.0 0.0 all-gather.7.cloned.1.call-update
  214.0 0.0 copy-done
  214.0 1.8 fusion.44
  215.8 0.7 broadcast_in_dim.31
  216.5 3.5 all-to-all-start.2
  220.1 92.0 %all-gather.7.cloned.1.call-done = bf16[1536,2304]{1,0:T(8,128)(2,1)} async-done(((bf16[192,2304]{1,0:T(8,128)(2,1)}), bf16[1536,2304]{1,0:T(8,128)(2,1)}) %all-gather.7.cloned.1.call-update) | async-done | bytes 7077904 | tf_op jit(solution)/shard_map/all_gather | solution.py:193
  312.1 7.3 %convolution_convert_fusion = bf16[2304,512]{1,0:T(8,128)(2,1)S(1)} fusion(bf16[1536,2304]{1,0:T(8,128)(2,1)} %all-gather.7.cloned.1.call-done, bf16[1,1536,512]{2,1,0:T(8,128)(2,1)} %param.13), kind=kOutput, calls=%fused_computation.21 | convolution fusion | flops 3625058304 | bytes 11010048 | tf_op jit(solution)/shard_map/dot_general | solution.py:194
  319.4 0.1 slice.66
  319.5 0.2 copy.57
  319.7 1.6 pad_maximum_fusion.1
  321.3 0.0 all-to-all-done.2
  321.3 8.7 %all-to-all-start.5 = ((bf16[32,72,512]{2,1,0:T(8,128)(2,1)}), bf16[32,72,512]{2,1,0:T(8,128)(2,1)}, u32[]{:S(2)}, u32[]{:S(2)}) async-start(bf16[32,72,512]{2,1,0:T(8,128)(2,1)} %pad_maximum_fusion.1), calls=%async_computation.5 | async-start | bytes 4718592 | tf_op jit(solution)/shard_map/all_to_all | solution.py:200
  330.0 0.1 broadcast_compare_fusion
  330.2 31.0 %all-to-all-done.5 = bf16[32,72,512]{2,1,0:T(8,128)(2,1)} async-done(((bf16[32,72,512]{2,1,0:T(8,128)(2,1)}), bf16[32,72,512]{2,1,0:T(8,128)(2,1)}, u32[]{:S(2)}, u32[]{:S(2)}) %all-to-all-start.5) | async-done | bytes 2359328 | tf_op jit(solution)/shard_map/all_to_all | solution.py:200
  361.2 5.4 %fusion.3 = f32[1024,512,1]{1,0,2:T(8,128)S(1)} fusion(bf16[32,72,512]{2,1,0:T(8,128)(2,1)} %all-to-all-done.5, f32[32,1024]{1,0:T(8,128)S(1)} %copy_bitcast_fusion.1, f32[32,1024]{1,0:T(8,128)S(1)} %bitcast.84, f32[72]{0:T(128)S(1)} %fusion.38, pred[72,1024]{1,0:T(8,128)(4,1)S(1)} %broadcast_compare_fusion), kind=kOutput, calls=%fused_computation.8 | convolution fusion | flops 2430074880 | bytes 4792608 | tf_op jit(solution)/shard_map/dot_general | solution.py:218
  366.6 4.8 %fusion.18 = bf16[1024,512]{1,0:T(8,128)(2,1)S(1)} fusion(f32[1024,512,1]{1,0,2:T(8,128)S(1)} %fusion.3, bf16[32,72,512]{2,1,0:T(8,128)(2,1)} %all-to-all-done.5, f32[32,1024]{1,0:T(8,128)S(1)} %copy_bitcast_fusion.1, f32[32,1024]{1,0:T(8,128)S(1)} %bitcast.85, f32[72]{0:T(128)S(1)} %fusion.38, pred[72,1024]{1,0:T(8,128)(4,1)S(1)} %broadcast_compare_fusion), kind=kOutput, calls=%fused_computation.28 | convolution fusion | flops 2428764160 | bytes 5841184 | tf_op jit(solution)/shard_map/dot_general | solution.py:217
  371.4 30.9 %all_to_all.37 = bf16[8,128,512]{2,1,0:T(8,128)(2,1)S(1)} all-to-all(bf16[8,128,512]{2,1,0:T(8,128)(2,1)S(1)} %bitcast.78), channel_id=1, replica_groups=mesh['dp'=32,'expert'=8] {'expert'}, dimensions={0} | all-to-all | bytes 2097152 | tf_op jit(solution)/shard_map/all_to_all | solution.py:220
  402.3 1.1 copy.51
  (18 shorter events, 0.2 us)
Async XLA Ops:
  6.5 207.4 %copy-start = (f32[4096,128]{1,0:T(8,128)S(1)}, f32[4096,128]{1,0:T(8,128)}, u32[]{:S(2)}) copy-start(f32[4096,128]{1,0:T(8,128)} %param.8) | copy-start | bytes 6291460
  6.5 21.8 %copy-start.4 = (bf16[128,4096]{1,0:T(8,128)(2,1)S(1)}, bf16[128,4096]{1,0:T(8,128)(2,1)}, u32[]{:S(2)}) copy-start(bf16[128,4096]{1,0:T(8,128)(2,1)} %param.7) | copy-start | bytes 3145732
  6.5 63.5 %all-gather.5.cloned.1.call-start = ((), (), s32[]{:S(2)}) async-start(), calls=%async_computation.7 | async-start | bytes 4128768 | tf_op jit(solution)/shard_map/all_gather | solution.py:133
  9.9 16.3 %all-to-all-start = ((s32[32,8,128]{2,1,0:T(8,128)}), s32[32,8,128]{2,1,0:T(8,128)S(1)}, u32[]{:S(2)}, u32[]{:S(2)}) async-start(s32[32,8,128]{2,1,0:T(8,128)} %broadcast_in_dim.26), calls=%async_computation | async-start | bytes 262144 | tf_op jit(solution)/shard_map/all_to_all | solution.py:138
  18.5 181.2 %all-gather.9.cloned.1.call-start = ((), (), s32[]{:S(2)}) async-start(), calls=%async_computation.9 | async-start | bytes 11943936 | tf_op jit(solution)/shard_map/all_gather | solution.py:175
  70.0 2.0 copy-start.2
  79.1 109.5 %all-to-all-start.4 = ((bf16[32,72,1792]{2,1,0:T(8,128)(2,1)}), bf16[32,72,1792]{2,1,0:T(8,128)(2,1)}, u32[]{:S(2)}, u32[]{:S(2)}) async-start(bf16[32,72,1792]{2,1,0:T(8,128)(2,1)} %shard_map.73), calls=%async_computation.4 | async-start | bytes 16515072 | tf_op jit(solution)/shard_map/all_to_all | solution.py:180
  85.2 226.8 %all-gather.7.cloned.1.call-start = ((), (), s32[]{:S(2)}) async-start(), calls=%async_computation.8 | async-start | bytes 7962624 | tf_op jit(solution)/shard_map/all_gather | solution.py:193
  95.6 2.1 copy-start.3
  199.7 1.7 copy-start.1
  216.5 104.8 %all-to-all-start.2 = ((f32[8,32,128]{2,1,0:T(8,128)}), f32[8,32,128]{2,1,0:T(8,128)S(1)}, u32[]{:S(2)}, u32[]{:S(2)}) async-start(f32[8,32,128]{2,1,0:T(8,128)} %broadcast_in_dim.31), calls=%async_computation.2 | async-start | bytes 262144 | tf_op jit(solution)/shard_map/all_to_all | solution.py:155
  321.3 39.9 %all-to-all-start.5 = ((bf16[32,72,512]{2,1,0:T(8,128)(2,1)}), bf16[32,72,512]{2,1,0:T(8,128)(2,1)}, u32[]{:S(2)}, u32[]{:S(2)}) async-start(bf16[32,72,512]{2,1,0:T(8,128)(2,1)} %pad_maximum_fusion.1), calls=%async_computation.5 | async-start | bytes 4718592 | tf_op jit(solution)/shard_map/all_to_all | solution.py:200
Sparse Core Ops, SparseCore 0:
  9.1 53.6 all-gather.4
  64.6 113.6 all-gather.8
  214.1 97.9 all-gather.6

commit v4 on v3

--- a/solution.py
+++ b/solution.py
@@ -8,8 +8,10 @@
 from jax.sharding import PartitionSpec as P
 
 MAIN = 8
-FIRST_WIDTH = 1792
-STEP = 256
+FIRST_WIDTH = 1408
+HIDDEN_STEPS = 3
+CUT = 4
+DISPATCH_STEPS = 1
 VMEM_BYTES = 48 * 1024 * 1024
 bf16, f32 = jnp.bfloat16, jnp.float32
 
@@ -56,12 +58,12 @@
     pairs = columns // 2
     return pl.pallas_call(
         functools.partial(first_dispatch_kernel, columns, tok_rows),
-        grid=(width // STEP,),
+        grid=(DISPATCH_STEPS,),
         in_specs=[
             pl.BlockSpec((owners, 1, row_toks), lambda f: (0, 0, 0)),
-            pl.BlockSpec((row_toks, STEP), lambda f: (0, f)),
-        ],
-        out_specs=pl.BlockSpec((owners, block_rows, STEP), lambda f: (0, 0, f)),
+            pl.BlockSpec((row_toks, width // DISPATCH_STEPS), lambda f: (0, f)),
+        ],
+        out_specs=pl.BlockSpec((owners, block_rows, width // DISPATCH_STEPS), lambda f: (0, 0, f)),
         out_shape=jax.ShapeDtypeStruct((owners, block_rows, width), bf16),
         scratch_shapes=[
             pltpu.VMEM((pairs, owners * 2 * MAIN, 2 * tok_rows), bf16),
@@ -71,48 +73,153 @@
     )(rank, raw)
 
 
-def hidden_kernel(main_steps, x_ref, w_ref, v_ref, o_ref):
-    columns, rows, width = x_ref.shape
+def hidden_kernel(rows, cut, x_ref, w_ref, v_ref, near_ref, far_ref, last_sum):
+    columns, step_rows, width = x_ref.shape
     half = w_ref.shape[1] // 2
-    acc = jnp.dot(x_ref[...].reshape(columns * rows, width), w_ref[...], preferred_element_type=f32)
-
-    def finish(acc):
-        val = acc + v_ref[...]
+    sources = rows // MAIN
+    hidden_part = near_ref.shape[0]
+    acc = jnp.dot(
+        x_ref[...].reshape(columns * step_rows, width), w_ref[...], preferred_element_type=f32
+    )
+
+    def store(ref, val, at):
         gate, up = val[:, :half], val[:, half:]
         hidden = gate / (1.0 + jnp.exp(-gate)) * up
-        o_ref[...] = hidden.T[: o_ref.shape[0]].astype(bf16)
-
-    @pl.when(pl.program_id(0) < main_steps)
-    def _():
-        pieces = [
-            acc[(j * rows + i) : (j * rows + i + MAIN)]
-            for i in range(0, rows, MAIN)
-            for j in range(columns)
-        ]
-        finish(jnp.concatenate(pieces, axis=0))
-
-    @pl.when(pl.program_id(0) == main_steps)
-    def _():
-        finish(acc)
-
-
-def hidden_rows(gathered, weight, first_val, hidden_part):
+        ref[:, at : at + val.shape[0]] = hidden.T[:hidden_part].astype(bf16)
+
+    def finish(step, blocks, with_last):
+        first_source = step * (step_rows // rows) * sources
+        for ref, lowest, highest in ((near_ref, 0, cut), (far_ref, cut, columns)):
+            count = (highest - lowest) * MAIN
+            pieces = [
+                acc[(j * step_rows + i) : (j * step_rows + i + MAIN)]
+                for i in range(0, blocks * rows, MAIN)
+                for j in range(lowest, highest)
+            ]
+            val = v_ref[first_source : first_source + blocks * sources, lowest * MAIN : highest * MAIN]
+            val = val.reshape(blocks * sources * count, 2 * half) + jnp.concatenate(pieces, axis=0)
+            store(ref, val, first_source * count)
+        if with_last:
+            for j in range(columns):
+                at = j * step_rows + blocks * rows
+                last_sum[j] = acc[at : at + rows]
+            val = jnp.concatenate([last_sum[:, i, :] for i in range(rows)], axis=0)
+            val = val + v_ref[:, columns * MAIN :].reshape(rows * columns, 2 * half)
+            store(far_ref, val, rows * (columns - cut) * MAIN)
+
+    for step in range(HIDDEN_STEPS):
+        blocks = step_rows // rows
+        with_last = step == HIDDEN_STEPS - 1
+        pl.when(pl.program_id(0) == step)(
+            functools.partial(finish, step, blocks - with_last, with_last)
+        )
+
+
+def hidden_rows(gathered, weight, first_val, hidden_part, cut):
     columns, col_rows, width = gathered.shape
-    steps = MAIN + 1
-    rows = col_rows // steps
-    step_rows = columns * rows
+    owners, block_rows, units = first_val.shape
+    steps = HIDDEN_STEPS
+    step_rows = col_rows // steps
+    near = owners * cut * MAIN
+    far = owners * block_rows - near
     return pl.pallas_call(
-        functools.partial(hidden_kernel, MAIN),
+        functools.partial(hidden_kernel, owners, cut),
         grid=(steps,),
         in_specs=[
-            pl.BlockSpec((columns, rows, width), lambda b: (0, b, 0)),
+            pl.BlockSpec((columns, step_rows, width), lambda b: (0, b, 0)),
             pl.BlockSpec(weight.shape, lambda b: (0, 0)),
-            pl.BlockSpec((step_rows, weight.shape[1]), lambda b: (b, 0)),
-        ],
-        out_specs=pl.BlockSpec((hidden_part, step_rows), lambda b: (0, b)),
-        out_shape=jax.ShapeDtypeStruct((hidden_part, steps * step_rows), bf16),
+            pl.BlockSpec(first_val.shape, lambda b: (0, 0, 0)),
+        ],
+        out_specs=[
+            pl.BlockSpec((hidden_part, near), lambda b: (0, 0)),
+            pl.BlockSpec((hidden_part, far), lambda b: (0, 0)),
+        ],
+        out_shape=[
+            jax.ShapeDtypeStruct((hidden_part, near), bf16),
+            jax.ShapeDtypeStruct((hidden_part, far), bf16),
+        ],
+        scratch_shapes=[pltpu.VMEM((columns, owners, units), f32)],
         compiler_params=pltpu.CompilerParams(vmem_limit_bytes=VMEM_BYTES),
     )(gathered, weight, first_val)
+
+
+def combine_kernel(columns, pair_high, pair_low, last_high, last_low, back_ref, out_ref):
+    owners, block_rows, width = back_ref.shape
+    pairs, pair_toks, pair_rows = pair_high.shape
+    rows = pair_rows // owners
+    last = back_ref[:, columns * MAIN :, :].reshape(owners * columns, width)
+    for pair in range(pairs):
+        back = back_ref[:, pair * rows : (pair + 1) * rows, :].reshape(pair_rows, width)
+        toks = slice(pair * pair_toks, (pair + 1) * pair_toks)
+        part = jnp.dot(pair_high[pair], back, preferred_element_type=f32)
+        part = part + jnp.dot(pair_low[pair], back, preferred_element_type=f32)
+        part = part + jnp.dot(last_high[toks], last, preferred_element_type=f32)
+        part = part + jnp.dot(last_low[toks], last, preferred_element_type=f32)
+        out_ref[toks] = part.astype(bf16)
+
+
+def combine(mats, back, columns):
+    row_toks = mats[2].shape[0]
+    return pl.pallas_call(
+        functools.partial(combine_kernel, columns),
+        out_shape=jax.ShapeDtypeStruct((row_toks, back.shape[2]), bf16),
+        compiler_params=pltpu.CompilerParams(vmem_limit_bytes=VMEM_BYTES),
+    )(*mats, back)
+
+
+def combine_matrices(rank, weight, columns, tok_rows):
+    row_toks, owners = rank.shape
+    high = lax.reduce_precision(weight, 8, 7)
+    parts = [high.astype(bf16), (weight - high).astype(bf16)]
+    column = jnp.arange(row_toks, dtype=jnp.int32)[:, None] // tok_rows
+
+    def matrix(count, row_column, row_slot):
+        lane = jnp.arange(owners * count, dtype=jnp.int32)
+        spread = (lane[None, :] // count == jnp.arange(owners, dtype=jnp.int32)[:, None]).astype(bf16)
+        wanted = jnp.where(row_column(column, lane % count), row_slot(lane % count), -2).astype(f32)
+        mine = jnp.dot(rank, spread, preferred_element_type=f32) == wanted
+        return [
+            jnp.where(mine, jnp.dot(p, spread, preferred_element_type=f32), 0.0).astype(bf16) for p in parts
+        ]
+
+    pairs = columns // 2
+    pair = matrix(2 * MAIN, lambda c, r: c % 2 == r[None] // MAIN, lambda r: r[None] % MAIN)
+    last = matrix(columns, lambda c, r: c == r[None], lambda r: MAIN)
+    return [m.reshape(pairs, 2 * tok_rows, owners * 2 * MAIN) for m in pair] + last
+
+
+def ordered(blocks):
+    columns = len(blocks)
+    me = lax.axis_index("expert")
+    out = jnp.zeros((columns,) + blocks[0].shape, blocks[0].dtype)
+    for distance, block in enumerate(blocks):
+        at = ((me + distance) % columns,) + (0,) * block.ndim
+        out = lax.dynamic_update_slice(out, block[None], at)
+    return out
+
+
+def gather_small(block):
+    columns = lax.axis_size("expert")
+    perms = [[((at + d) % columns, at) for at in range(columns)] for d in range(1, columns)]
+    return ordered([block] + [lax.ppermute(block, "expert", perm) for perm in perms])
+
+
+def gather_ring(block):
+    columns = lax.axis_size("expert")
+    rise = [(at, (at + 1) % columns) for at in range(columns)]
+    fall = [(at, (at - 1) % columns) for at in range(columns)]
+    below, above = block, block
+    blocks = {0: block}
+    for distance in range(1, columns // 2):
+        below = lax.ppermute(below, "expert", rise)
+        above = lax.ppermute(above, "expert", fall)
+        blocks[columns - distance] = below
+        blocks[distance] = above
+    middle = block.shape[0] // 2
+    below = lax.ppermute(below[:middle], "expert", rise)
+    above = lax.ppermute(above[middle:], "expert", fall)
+    blocks[columns // 2] = jnp.concatenate([below, above], axis=0)
+    return ordered([blocks[at] for at in range(columns)])
 
 
 def per_device(tokens, router_weight, rollout_ids, source_row, gate_weight, up_weight, down_weight):
@@ -128,7 +235,6 @@
     first = FIRST_WIDTH
     second = model_width - first
     fold = -(-second // (MAIN * 128)) * 128
-    main_rows = owners * columns * MAIN
 
     raw = lax.all_gather(tokens[:, :first], "expert", axis=0, tiled=True)
 
@@ -150,13 +256,8 @@
     slot_rank = jnp.dot(before.astype(bf16), chosen.astype(bf16), preferred_element_type=f32)
     slot_rank = jnp.where(chosen, slot_rank, -1.0)
 
-    def whole_row(info):
-        sent = jnp.broadcast_to(info.T[None], (columns, owners, tok_rows))
-        got = lax.all_to_all(sent, "expert", split_axis=0, concat_axis=0, tiled=True)
-        return jnp.transpose(got, (1, 0, 2)).reshape(owners, 1, row_toks)
-
-    row_rank = whole_row(slot_rank.astype(bf16)).astype(f32)
-
+    raised = jnp.where(picks, jnp.exp(jnp.where(picks, logits, 0.0)), 0.0)
+    weights = raised / jnp.sum(raised, axis=1, keepdims=True)
     def select(lowest, count):
         slots = jnp.arange(lowest, lowest + count, dtype=f32)
         sel = slot_rank[:, :, None] == slots
@@ -170,6 +271,12 @@
     sent_last = sent_last.reshape(owners, MAIN, fold)
     sent = jnp.concatenate([sent_main, sent_last], axis=2)
     arrived = lax.all_to_all(sent, "dp", split_axis=0, concat_axis=0, tiled=True)
+    arrived, rank = lax.optimization_barrier((arrived, slot_rank.T.astype(bf16)))
+    rank = lax.all_to_all(
+        jnp.broadcast_to(rank[None], (columns,) + rank.shape), "expert", 0, 0, tiled=True
+    )
+    row_rank = jnp.transpose(rank, (1, 0, 2)).astype(f32).reshape(owners, 1, row_toks)
+    tok_rank = jnp.transpose(rank, (0, 2, 1)).reshape(row_toks, owners)
     arrived_main = arrived[:, :, :second].reshape(owners * MAIN, second)
     arrived_last = arrived[:, :, second:].reshape(owners, MAIN * fold)[:, :second]
     gathered = lax.all_gather(
@@ -177,6 +284,7 @@
     )
 
     first_sent = first_dispatch(row_rank, raw, columns, tok_rows)
+    weights, first_sent = lax.optimization_barrier((weights[:, :owners].T, first_sent))
     first_rows = lax.all_to_all(first_sent, "dp", split_axis=0, concat_axis=0, tiled=True)
 
     half = -(-hidden_part // 128) * 128
@@ -185,38 +293,30 @@
     first_val = jnp.dot(
         first_rows.reshape(slot_rows, first), both[:first], preferred_element_type=f32
     ).reshape(owners, block_rows, 2 * half)
-    first_main = first_val[:, : columns * MAIN].reshape(main_rows, 2 * half)
-    first_last = jnp.transpose(first_val[:, columns * MAIN :], (1, 0, 2))
-    first_val = jnp.concatenate([first_main, first_last.reshape(-1, 2 * half)], axis=0)
-
-    hidden = hidden_rows(gathered, both[first:], first_val, hidden_part)
-    full = lax.all_gather(hidden, "expert", axis=0, tiled=True)
-    out = lax.dot_general(
-        full, down_weight[0], (((0,), (0,)), ((), ())), preferred_element_type=f32
-    ).astype(bf16)
-    out_main = out[:main_rows].reshape(owners, columns * MAIN, out_width)
-    out_last = jnp.transpose(out[main_rows:].reshape(columns, owners, out_width), (1, 0, 2))
-    out = jnp.concatenate([out_main, out_last], axis=1)
+    tok_weight = jnp.transpose(gather_small(weights), (0, 2, 1)).reshape(row_toks, owners)
+    mats = combine_matrices(tok_rank, tok_weight, columns, tok_rows)
+    mats, first_val = lax.optimization_barrier((mats, first_val))
+
+    near, far = hidden_rows(gathered, both[first:], first_val, hidden_part, CUT)
+    far = lax.all_gather(far, "expert", axis=0, tiled=True)
+    near = gather_ring(near).reshape(columns * hidden_part, -1)
+
+    def project(full):
+        out = lax.dot_general(full, down_weight[0], (((0,), (0,)), ((), ())), preferred_element_type=f32)
+        return out.astype(bf16)
+
+    far_main = owners * (columns - CUT) * MAIN
+    near, far = project(near), project(far)
+    out = jnp.concatenate(
+        [
+            near.reshape(owners, -1, out_width),
+            far[:far_main].reshape(owners, -1, out_width),
+            far[far_main:].reshape(owners, columns, out_width),
+        ],
+        axis=1,
+    )
     back = lax.all_to_all(out, "dp", split_axis=0, concat_axis=0, tiled=True)
-    back = back.reshape(slot_rows, out_width)
-
-    raised = jnp.where(picks, jnp.exp(jnp.where(picks, logits, 0.0)), 0.0)
-    weights = raised / jnp.sum(raised, axis=1, keepdims=True)
-    row_weight = whole_row(weights[:, :owners])
-    row = jnp.arange(block_rows, dtype=jnp.int32)
-    is_main = row < columns * MAIN
-    row_column = jnp.where(is_main, row // MAIN, row - columns * MAIN)
-    row_slot = jnp.where(is_main, row % MAIN, MAIN).astype(f32)
-    tok_column = jnp.arange(row_toks, dtype=jnp.int32) // tok_rows
-    same_column = row_column[:, None] == tok_column[None, :]
-    taken = (row_rank == row_slot[None, :, None]) & same_column[None]
-    mat = jnp.where(taken, row_weight, 0.0).reshape(slot_rows, row_toks)
-    high = lax.reduce_precision(mat, 8, 7)
-    low = (mat - high).astype(bf16)
-    dims = (((0,), (0,)), ((), ()))
-    part = lax.dot_general(high.astype(bf16), back, dims, preferred_element_type=f32)
-    part = part + lax.dot_general(low, back, dims, preferred_element_type=f32)
-    part = part.astype(bf16).reshape(columns, tok_rows, out_width)
+    part = combine(mats, back, columns).reshape(columns, tok_rows, out_width)
     whole = lax.all_to_all(part, "expert", split_axis=0, concat_axis=0, tiled=True)
     return jnp.transpose(whole, (1, 0, 2)).reshape(tok_rows, model_width)
 

time: 411 us -> 371 us (0.903)
  waiting for transfers between devices: 217 us -> 153 us
  starting transfers between devices: 27 us -> 48.4 us
    all_gather x1, waiting for transfers between devices: 92 us -> 7.96 us  [per_device(): far = lax.all_gather(far, 'expert', axis=0, tiled=True)]
    ppermute x0 -> x15, waiting for transfers between devices: none -> 54.9 us  [the longest x3 24.1 us: gather_ring(): above = lax.ppermute(above, 'expert', fall)]
    all_to_all x1, waiting for transfers between devices: 89.4 us -> 42.9 us  [per_device(): lax.all_to_all(first_sent, 'dp', split_axis=0, concat_axis=0, tiled=True)]
    ppermute x0 -> x15, starting transfers between devices: none -> 19.8 us  [the longest x7 9.48 us: gather_small(): lax.ppermute(block, 'expert', perm)]
    all_gather x1, waiting for transfers between devices: 0.01 us -> 12.6 us  [per_device(): lax.all_gather(jnp.concatenate([arrived_main, arrived_last], axis=0), 'ex...]
    unnamed x14 -> x28, local copies, waits for them, and re-layouts: 13.5 us -> 10.5 us
    pallas_call x1 -> x2, Pallas kernels: 12.6 us -> 15.5 us  [the longest x1 11.9 us: hidden_rows(): pl.pallas_call(functools.partial(hidden_kernel, owners, cut), grid=(steps...]
    all_to_all x2 -> x1, blocking collectives: 39.6 us -> 37.6 us  [per_device(): back = lax.all_to_all(out, 'dp', split_axis=0, concat_axis=0, tiled=True)]
  transfers between devices with their start and end apart: 7 -> 22, of which waited for: 4 -> 13; matrix products, arithmetic and copies ran while one was open for 10% -> 13% of each run, Pallas kernels for 2% -> 1%
where the time goes in v4:
time: 371 us; the launch traced here: 370 us
  waiting for transfers between devices  153 us (41%)
  blocking collectives  71.6 us (19%)
  starting transfers between devices  48.4 us (13%)
  matrix products  30.4 us (8%)
  local copies, waits for them, and re-layouts  21.6 us (6%)
  Pallas kernels  20.9 us (6%)
  between operations  16.4 us (4%)
  other arithmetic  7.54 us (2%)
    all_to_all x1, waiting for transfers between devices, per_device(): lax.all_to_all(first_sent, 'dp', split_axis=0, concat_axis=0, tiled=True)  42.9 us
    all_to_all x1, blocking collectives, per_device(): back = lax.all_to_all(out, 'dp', split_axis=0, concat_axis=0, tiled=True)  37.6 us
    all_to_all x1, blocking collectives, per_device(): lax.all_to_all(part, 'expert', split_axis=0, concat_axis=0, tiled=True)  34 us
    ppermute x3, waiting for transfers between devices, gather_ring(): above = lax.ppermute(above, 'expert', fall)  24.1 us
    all_to_all x1, waiting for transfers between devices, per_device(): lax.all_to_all(sent, 'dp', split_axis=0, concat_axis=0, tiled=True)  22.8 us
    ppermute x3, waiting for transfers between devices, gather_ring(): below = lax.ppermute(below, 'expert', rise)  19.2 us
    all_gather x1, waiting for transfers between devices, per_device(): lax.all_gather(jnp.concatenate([arrived_main, arrived_last], axis=0), 'ex...  12.6 us
    pallas_call x1, Pallas kernels, hidden_rows(): pl.pallas_call(functools.partial(hidden_kernel, owners, cut), grid=(steps...  11.9 us
  transfers between devices with their start and end apart: 22, of which 13 were waited for; matrix products, arithmetic and copies ran while one was open for 13% of the time, Pallas kernels for 1%

profile of v4, /device:TPU:1, one launch (start us, length us, event | category | flops | bytes accessed | tf_op | source)
XLA Modules:
  0.0 369.7 jit_solution(3864902053945979601)
XLA Ops:
  6.5 1.9 slice.47
  8.5 1.3 broadcast_in_dim.123
  9.8 8.6 %all-to-all-start = ((s32[32,8,128]{2,1,0:T(8,128)}), s32[32,8,128]{2,1,0:T(8,128)S(1)}, u32[]{:S(2)}, u32[]{:S(2)}) async-start(s32[32,8,128]{2,1,0:T(8,128)} %broadcast_in_dim.123), calls=%async_computation | async-start | bytes 262144 | tf_op jit(solution)/shard_map/all_to_all | solution.py:244
  21.1 0.7 and_select_fusion.2
  21.8 4.3 %all-to-all-done = s32[32,8,128]{2,1,0:T(8,128)S(1)} async-done(((s32[32,8,128]{2,1,0:T(8,128)}), s32[32,8,128]{2,1,0:T(8,128)S(1)}, u32[]{:S(2)}, u32[]{:S(2)}) %all-to-all-start) | async-done | bytes 131104 | tf_op jit(solution)/shard_map/all_to_all | solution.py:244
  26.3 0.3 fusion.17
  26.9 1.3 convolution_convert_fusion.1
  28.3 0.6 fusion.3
  28.8 1.4 pad_maximum_fusion.1
  30.2 4.7 %all-to-all-start.1 = ((bf16[32,8,3072]{2,1,0:T(8,128)(2,1)}), bf16[32,8,3072]{2,1,0:T(8,128)(2,1)}, u32[]{:S(2)}, u32[]{:S(2)}) async-start(bf16[32,8,3072]{2,1,0:T(8,128)(2,1)} %pad_maximum_fusion.1), calls=%async_computation.1 | async-start | bytes 3145728 | tf_op jit(solution)/shard_map/all_to_all | solution.py:273
  35.0 22.8 %all-to-all-done.1 = bf16[32,8,3072]{2,1,0:T(8,128)(2,1)} async-done(((bf16[32,8,3072]{2,1,0:T(8,128)(2,1)}), bf16[32,8,3072]{2,1,0:T(8,128)(2,1)}, u32[]{:S(2)}, u32[]{:S(2)}) %all-to-all-start.1) | async-done | bytes 1572896 | tf_op jit(solution)/shard_map/all_to_all | solution.py:273
  57.7 0.9 slice.50
  58.7 1.4 slice_bitcast_fusion.2
  60.2 1.2 pad_maximum_fusion.2
  61.5 1.8 fusion.57
  63.3 0.6 broadcast_in_dim.125
  63.9 8.2 %all-to-all-start.2 = ((bf16[8,32,128]{2,1,0:T(8,128)(2,1)}), bf16[8,32,128]{2,1,0:T(8,128)(2,1)S(1)}, u32[]{:S(2)}, u32[]{:S(2)}) async-start(bf16[8,32,128]{2,1,0:T(8,128)(2,1)} %broadcast_in_dim.125), calls=%async_computation.2 | async-start | bytes 131072 | tf_op jit(solution)/shard_map/all_to_all | solution.py:275
  72.1 7.5 %all-to-all-done.2 = bf16[8,32,128]{2,1,0:T(8,128)(2,1)S(1)} async-done(((bf16[8,32,128]{2,1,0:T(8,128)(2,1)}), bf16[8,32,128]{2,1,0:T(8,128)(2,1)S(1)}, u32[]{:S(2)}, u32[]{:S(2)}) %all-to-all-start.2) | async-done | bytes 65568 | tf_op jit(solution)/shard_map/all_to_all | solution.py:275
  79.8 1.8 copy-done.4
  81.6 5.4 %shard_map.73 = bf16[32,72,1408]{2,1,0:T(8,128)(2,1)} custom-call(f32[32,1,1024]{2,1,0:T(1,128)S(1)} %bitcast.122, bf16[1024,1408]{1,0:T(8,128)(2,1)S(1)} %copy-done.4), custom_call_target="tpu_custom_call" | custom-call | tf_op jit(solution)/shard_map/pallas_call | solution.py:59
  86.9 7.1 %all-to-all-start.3 = ((bf16[32,72,1408]{2,1,0:T(8,128)(2,1)}), bf16[32,72,1408]{2,1,0:T(8,128)(2,1)}, u32[]{:S(2)}, u32[]{:S(2)}) async-start(bf16[32,72,1408]{2,1,0:T(8,128)(2,1)} %shard_map.73), calls=%async_computation.3 | async-start | bytes 12976128 | tf_op jit(solution)/shard_map/all_to_all | solution.py:288
  94.2 3.2 copy.66
  97.3 3.8 %copy.67 = bf16[1,4096,192]{2,1,0:T(8,128)(2,1)} copy(bf16[1,4096,192]{1,2,0:T(8,128)(2,1)} %param.12) | data formatting | bytes 3145728 | tf_op args[5]
  101.2 3.7 %fusion.2 = bf16[4096,512]{1,0:T(8,128)(2,1)} fusion(bf16[4096,192]{1,0:T(8,128)(2,1)} %bitcast.125, bf16[4096,192]{1,0:T(8,128)(2,1)S(1)} %bitcast.124), kind=kLoop, calls=%fused_computation.4 | loop fusion | flops 16777216 | bytes 7340032 | tf_op jit(solution)/shard_map/concatenate | solution.py:292
  104.9 2.0 slice.61.w_ref
  107.0 0.2 collective-permute-start
  107.2 0.2 collective-permute-start.1
  107.4 1.5 convert_compare_fusion
  108.8 3.3 collective-permute-start.2
  112.2 2.2 collective-permute-start.3
  114.3 2.2 collective-permute-start.4
  116.5 1.2 collective-permute-start.5
  117.9 1.1 convolution_compare_fusion
  119.5 1.4 collective-permute-done.4
  120.9 1.1 collective-permute-done.5
  122.1 1.1 collective-permute-done.6
  123.3 1.3 fusion.12.last_low
  124.6 2.1 fusion.11.last_high
  126.7 2.5 select_convert_fusion
  129.2 2.5 select_convert_fusion.1
  131.7 42.9 %all-to-all-done.3 = bf16[32,72,1408]{2,1,0:T(8,128)(2,1)} async-done(((bf16[32,72,1408]{2,1,0:T(8,128)(2,1)}), bf16[32,72,1408]{2,1,0:T(8,128)(2,1)}, u32[]{:S(2)}, u32[]{:S(2)}) %all-to-all-start.3) | async-done | bytes 6488096 | tf_op jit(solution)/shard_map/all_to_all | solution.py:288
  174.6 9.3 %fusion.10.v_ref = f32[32,72,512]{2,1,0:T(8,128)} fusion(bf16[32,72,1408]{2,1,0:T(8,128)(2,1)} %all-to-all-done.3, bf16[4096,512]{1,0:T(8,128)(2,1)} %fusion.2), kind=kOutput, calls=%fused_computation.20 | convolution fusion | flops 3321888768 | bytes 12648448 | tf_op jit(solution)/shard_map/dot_general | solution.py:293
  183.9 12.6 %all-gather.9.cloned.1.call-done = bf16[2304,2688]{1,0:T(8,128)(2,1)} async-done(((bf16[288,2688]{1,0:T(8,128)(2,1)}), bf16[2304,2688]{1,0:T(8,128)(2,1)}) %all-gather.9.cloned.1.call-update) | async-done | bytes 12386320 | tf_op jit(solution)/shard_map/all_gather | solution.py:282
  196.5 11.9 %shard_map.74 = (bf16[192,1024]{1,0:T(8,128)(2,1)S(1)}, bf16[192,1280]{1,0:T(8,128)(2,1)S(1)}) custom-call(bf16[8,288,2688]{2,1,0:T(8,128)(2,1)} %bitcast.123, bf16[2688,512]{1,0:T(8,128)(2,1)S(1)} %slice.61.w_ref, f32[32,72,512]{2,1,0:T(8,128)} %fusion.10.v_ref), custom_call_target="tpu_custom_call" | custom-call | tf_op jit(solution)/shard_map/pallas_call | solution.py:125
  208.4 0.8 copy-done.6
  209.2 0.8 copy-done.7
  210.0 1.2 collective-permute-start.7
  211.1 0.4 collective-permute-start.10
  211.5 8.7 %collective-permute-done.7 = bf16[192,1024]{1,0:T(8,128)(2,1)S(1)} collective-permute-done((bf16[192,1024]{1,0:T(8,128)(2,1)}, bf16[192,1024]{1,0:T(8,128)(2,1)S(1)}, u32[]{:S(2)}, u32[]{:S(2)}) %collective-permute-start.7) | collective-permute-done | bytes 393248 | tf_op jit(solution)/shard_map/ppermute | solution.py:215
  220.2 2.5 collective-permute-start.8
  222.7 0.4 broadcast_in_dim.142
  223.2 15.4 %collective-permute-done.8 = bf16[192,1024]{1,0:T(8,128)(2,1)S(1)} collective-permute-done((bf16[192,1024]{1,0:T(8,128)(2,1)S(1)}, bf16[192,1024]{1,0:T(8,128)(2,1)S(1)}, u32[]{:S(2)}, u32[]{:S(2)}) %collective-permute-start.8) | collective-permute-done | bytes 393248 | tf_op jit(solution)/shard_map/ppermute | solution.py:215
  238.6 3.5 collective-permute-start.9
  242.2 19.2 %collective-permute-done.12 = bf16[192,1024]{1,0:T(8,128)(2,1)S(1)} collective-permute-done((bf16[192,1024]{1,0:T(8,128)(2,1)S(1)}, bf16[192,1024]{1,0:T(8,128)(2,1)S(1)}, u32[]{:S(2)}, u32[]{:S(2)}) %collective-permute-start.12) | collective-permute-done | bytes 393248 | tf_op jit(solution)/shard_map/ppermute | solution.py:214
  261.5 2.7 collective-permute-start.14
  264.2 8.0 %collective-permute-done.13 = bf16[96,1024]{1,0:T(8,128)(2,1)S(1)} collective-permute-done((bf16[96,1024]{1,0:T(8,128)(2,1)S(1)}, bf16[96,1024]{1,0:T(8,128)(2,1)S(1)}, u32[]{:S(2)}, u32[]{:S(2)}) %collective-permute-start.13) | collective-permute-done | bytes 196640 | tf_op jit(solution)/shard_map/ppermute | solution.py:219
  272.4 1.8 fusion.7
  274.2 8.0 %all-gather.7.cloned.1.call-done = bf16[1536,1280]{1,0:T(8,128)(2,1)} async-done(((bf16[192,1280]{1,0:T(8,128)(2,1)}), bf16[1536,1280]{1,0:T(8,128)(2,1)}) %all-gather.7.cloned.1.call-update) | async-done | bytes 3932176 | tf_op jit(solution)/shard_map/all_gather | solution.py:301
  282.2 4.3 %convolution_convert_fusion.2 = bf16[1280,512]{1,0:T(8,128)(2,1)S(1)} fusion(bf16[1536,1280]{1,0:T(8,128)(2,1)} %all-gather.7.cloned.1.call-done, bf16[1,1536,512]{2,1,0:T(8,128)(2,1)S(1)} %copy-done.11), kind=kOutput, calls=%fused_computation.8 | convolution fusion | flops 2013921280 | bytes 6815744 | tf_op jit(solution)/shard_map/dot_general | solution.py:305
  286.7 0.2 pad_maximum_fusion
  286.9 37.6 %all_to_all.30.back_ref = bf16[32,72,512]{2,1,0:T(8,128)(2,1)} all-to-all(bf16[32,72,512]{2,1,0:T(8,128)(2,1)S(1)} %pad_maximum_fusion), channel_id=1, replica_groups=mesh['dp'=32,'expert'=8] {'dp'}, dimensions={0} | all-to-all | bytes 4718592 | tf_op jit(solution)/shard_map/all_to_all | solution.py:318
  324.6 3.6 shard_map.75
  328.2 34.0 %all_to_all.31 = bf16[8,128,512]{2,1,0:T(8,128)(2,1)S(1)} all-to-all(bf16[8,128,512]{2,1,0:T(8,128)(2,1)S(1)} %bitcast.121), channel_id=1, replica_groups=mesh['dp'=32,'expert'=8] {'expert'}, dimensions={0} | all-to-all | bytes 2097152 | tf_op jit(solution)/shard_map/all_to_all | solution.py:320
  362.1 1.1 copy.70
  (80 shorter events, 2.3 us)
Async XLA Ops:
  6.5 54.9 %copy-start = (f32[4096,128]{1,0:T(8,128)S(1)}, f32[4096,128]{1,0:T(8,128)}, u32[]{:S(2)}) copy-start(f32[4096,128]{1,0:T(8,128)} %param.8) | copy-start | bytes 6291460
  6.5 21.7 %copy-start.9 = (bf16[128,4096]{1,0:T(8,128)(2,1)S(1)}, bf16[128,4096]{1,0:T(8,128)(2,1)}, u32[]{:S(2)}) copy-start(bf16[128,4096]{1,0:T(8,128)(2,1)} %param.7) | copy-start | bytes 3145732
  6.5 73.2 %all-gather.5.cloned.1.call-start = ((), (), s32[]{:S(2)}) async-start(), calls=%async_computation.6 | async-start | bytes 3244032 | tf_op jit(solution)/shard_map/all_gather | solution.py:239
  9.8 16.3 %all-to-all-start = ((s32[32,8,128]{2,1,0:T(8,128)}), s32[32,8,128]{2,1,0:T(8,128)S(1)}, u32[]{:S(2)}, u32[]{:S(2)}) async-start(s32[32,8,128]{2,1,0:T(8,128)} %broadcast_in_dim.123), calls=%async_computation | async-start | bytes 262144 | tf_op jit(solution)/shard_map/all_to_all | solution.py:244
  30.2 27.5 %all-to-all-start.1 = ((bf16[32,8,3072]{2,1,0:T(8,128)(2,1)}), bf16[32,8,3072]{2,1,0:T(8,128)(2,1)}, u32[]{:S(2)}, u32[]{:S(2)}) async-start(bf16[32,8,3072]{2,1,0:T(8,128)(2,1)} %pad_maximum_fusion.1), calls=%async_computation.1 | async-start | bytes 3145728 | tf_op jit(solution)/shard_map/all_to_all | solution.py:273
  34.9 161.6 %all-gather.9.cloned.1.call-start = ((), (), s32[]{:S(2)}) async-start(), calls=%async_computation.8 | async-start | bytes 13934592 | tf_op jit(solution)/shard_map/all_gather | solution.py:282
  63.9 15.7 %all-to-all-start.2 = ((bf16[8,32,128]{2,1,0:T(8,128)(2,1)}), bf16[8,32,128]{2,1,0:T(8,128)(2,1)S(1)}, u32[]{:S(2)}, u32[]{:S(2)}) async-start(bf16[8,32,128]{2,1,0:T(8,128)(2,1)} %broadcast_in_dim.125), calls=%async_computation.2 | async-start | bytes 131072 | tf_op jit(solution)/shard_map/all_to_all | solution.py:275
  79.8 1.8 copy-start.4
  86.9 87.6 %all-to-all-start.3 = ((bf16[32,72,1408]{2,1,0:T(8,128)(2,1)}), bf16[32,72,1408]{2,1,0:T(8,128)(2,1)}, u32[]{:S(2)}, u32[]{:S(2)}) async-start(bf16[32,72,1408]{2,1,0:T(8,128)(2,1)} %shard_map.73), calls=%async_computation.3 | async-start | bytes 12976128 | tf_op jit(solution)/shard_map/all_to_all | solution.py:288
  94.0 188.2 %all-gather.7.cloned.1.call-start = ((), (), s32[]{:S(2)}) async-start(), calls=%async_computation.7 | async-start | bytes 4423680 | tf_op jit(solution)/shard_map/all_gather | solution.py:301
  107.0 9.6 %collective-permute-start = (f32[32,128]{1,0:T(8,128)S(1)}, f32[32,128]{1,0:T(8,128)S(1)}, u32[]{:S(2)}, u32[]{:S(2)}) collective-permute-start(f32[32,128]{1,0:T(8,128)S(1)} %fusion.30), channel_id=1, source_target_pairs={{1,0},{2,1},{3,2},{4,3},{5,4},{6,5},{7,6},{0,7},{9,8},{10,9},{11,1... | collective-permute-start | bytes 49160 | tf_op jit(solution)/shard_map/ppermute | solution.py:204
  107.2 10.6 %collective-permute-start.1 = (f32[32,128]{1,0:T(8,128)S(1)}, f32[32,128]{1,0:T(8,128)S(1)}, u32[]{:S(2)}, u32[]{:S(2)}) collective-permute-start(f32[32,128]{1,0:T(8,128)S(1)} %fusion.30), channel_id=1, source_target_pairs={{2,0},{3,1},{4,2},{5,3},{6,4},{7,5},{0,6},{1,7},{10,8},{11,9},{12,... | collective-permute-start | bytes 49160 | tf_op jit(solution)/shard_map/ppermute | solution.py:204
  108.8 10.5 %collective-permute-start.2 = (f32[32,128]{1,0:T(8,128)S(1)}, f32[32,128]{1,0:T(8,128)S(1)}, u32[]{:S(2)}, u32[]{:S(2)}) collective-permute-start(f32[32,128]{1,0:T(8,128)S(1)} %fusion.30), channel_id=1, source_target_pairs={{3,0},{4,1},{5,2},{6,3},{7,4},{0,5},{1,6},{2,7},{11,8},{12,9},{13,... | collective-permute-start | bytes 49160 | tf_op jit(solution)/shard_map/ppermute | solution.py:204
  112.2 7.2 %collective-permute-start.3 = (f32[32,128]{1,0:T(8,128)S(1)}, f32[32,128]{1,0:T(8,128)S(1)}, u32[]{:S(2)}, u32[]{:S(2)}) collective-permute-start(f32[32,128]{1,0:T(8,128)S(1)} %fusion.30), channel_id=1, source_target_pairs={{4,0},{5,1},{6,2},{7,3},{0,4},{1,5},{2,6},{3,7},{12,8},{13,9},{14,... | collective-permute-start | bytes 49160 | tf_op jit(solution)/shard_map/ppermute | solution.py:204
  114.3 6.5 %collective-permute-start.4 = (f32[32,128]{1,0:T(8,128)S(1)}, f32[32,128]{1,0:T(8,128)S(1)}, u32[]{:S(2)}, u32[]{:S(2)}) collective-permute-start(f32[32,128]{1,0:T(8,128)S(1)} %fusion.30), channel_id=1, source_target_pairs={{5,0},{6,1},{7,2},{0,3},{1,4},{2,5},{3,6},{4,7},{13,8},{14,9},{15,... | collective-permute-start | bytes 49160 | tf_op jit(solution)/shard_map/ppermute | solution.py:204
  116.5 5.5 %collective-permute-start.5 = (f32[32,128]{1,0:T(8,128)S(1)}, f32[32,128]{1,0:T(8,128)S(1)}, u32[]{:S(2)}, u32[]{:S(2)}) collective-permute-start(f32[32,128]{1,0:T(8,128)S(1)} %fusion.30), channel_id=1, source_target_pairs={{6,0},{7,1},{0,2},{1,3},{2,4},{3,5},{4,6},{5,7},{14,8},{15,9},{8,1... | collective-permute-start | bytes 49160 | tf_op jit(solution)/shard_map/ppermute | solution.py:204
  117.8 5.5 %collective-permute-start.6 = (f32[32,128]{1,0:T(8,128)S(1)}, f32[32,128]{1,0:T(8,128)S(1)}, u32[]{:S(2)}, u32[]{:S(2)}) collective-permute-start(f32[32,128]{1,0:T(8,128)S(1)} %fusion.30), channel_id=1, source_target_pairs={{7,0},{0,1},{1,2},{2,3},{3,4},{4,5},{5,6},{6,7},{15,8},{8,9},{9,10... | collective-permute-start | bytes 49160 | tf_op jit(solution)/shard_map/ppermute | solution.py:204
  208.4 0.8 copy-start.6
  209.2 0.8 copy-start.7
  210.0 13.2 %copy-start.8 = (bf16[192,1024]{1,0:T(8,128)(2,1)S(1)}, bf16[192,1024]{1,0:T(8,128)(2,1)}, u32[]{:S(2)}) copy-start(bf16[192,1024]{1,0:T(8,128)(2,1)} %copy-done.7) | copy-start | bytes 1179652
  210.0 10.2 %collective-permute-start.7 = (bf16[192,1024]{1,0:T(8,128)(2,1)}, bf16[192,1024]{1,0:T(8,128)(2,1)S(1)}, u32[]{:S(2)}, u32[]{:S(2)}) collective-permute-start(bf16[192,1024]{1,0:T(8,128)(2,1)} %copy-done.7), channel_id=1, source_target_pairs={{0,7},{1,0},{2,1},{3,2},{4,3},{5,4},{6,5},{7,6},{8,15},{9,8},{10,9... | collective-permute-start | bytes 1179656 | tf_op jit(solution)/shard_map/ppermute | solution.py:215
  211.1 11.6 %collective-permute-start.10 = (bf16[192,1024]{1,0:T(8,128)(2,1)}, bf16[192,1024]{1,0:T(8,128)(2,1)S(1)}, u32[]{:S(2)}, u32[]{:S(2)}) collective-permute-start(bf16[192,1024]{1,0:T(8,128)(2,1)} %copy-done.7), channel_id=1, source_target_pairs={{0,1},{1,2},{2,3},{3,4},{4,5},{5,6},{6,7},{7,0},{8,9},{9,10},{10,1... | collective-permute-start | bytes 1179656 | tf_op jit(solution)/shard_map/ppermute | solution.py:214
  220.2 18.4 %collective-permute-start.8 = (bf16[192,1024]{1,0:T(8,128)(2,1)S(1)}, bf16[192,1024]{1,0:T(8,128)(2,1)S(1)}, u32[]{:S(2)}, u32[]{:S(2)}) collective-permute-start(bf16[192,1024]{1,0:T(8,128)(2,1)S(1)} %collective-permute-done.7), channel_id=1, source_target_pairs={{0,7},{1,0},{2,1},{3,2},{4,3},{5,4},{6,5},{7,6},{8,15},{9,8},{10,9... | collective-permute-start | bytes 1179656 | tf_op jit(solution)/shard_map/ppermute | solution.py:215
  222.7 19.3 %collective-permute-start.11 = (bf16[192,1024]{1,0:T(8,128)(2,1)S(1)}, bf16[192,1024]{1,0:T(8,128)(2,1)S(1)}, u32[]{:S(2)}, u32[]{:S(2)}) collective-permute-start(bf16[192,1024]{1,0:T(8,128)(2,1)S(1)} %collective-permute-done.10), channel_id=1, source_target_pairs={{0,1},{1,2},{2,3},{3,4},{4,5},{5,6},{6,7},{7,0},{8,9},{9,10},{10,1... | collective-permute-start | bytes 1179656 | tf_op jit(solution)/shard_map/ppermute | solution.py:214
  223.2 49.2 %copy-start.10 = (bf16[1,1536,512]{2,1,0:T(8,128)(2,1)S(1)}, bf16[1,1536,512]{2,1,0:T(8,128)(2,1)}, u32[]{:S(2)}) copy-start(bf16[1,1536,512]{2,1,0:T(8,128)(2,1)} %param.13) | copy-start | bytes 4718596
  238.6 22.8 %collective-permute-start.9 = (bf16[192,1024]{1,0:T(8,128)(2,1)S(1)}, bf16[192,1024]{1,0:T(8,128)(2,1)S(1)}, u32[]{:S(2)}, u32[]{:S(2)}) collective-permute-start(bf16[192,1024]{1,0:T(8,128)(2,1)S(1)} %collective-permute-done.8), channel_id=1, source_target_pairs={{0,7},{1,0},{2,1},{3,2},{4,3},{5,4},{6,5},{7,6},{8,15},{9,8},{10,9... | collective-permute-start | bytes 1179656 | tf_op jit(solution)/shard_map/ppermute | solution.py:215
  242.1 19.2 %collective-permute-start.12 = (bf16[192,1024]{1,0:T(8,128)(2,1)S(1)}, bf16[192,1024]{1,0:T(8,128)(2,1)S(1)}, u32[]{:S(2)}, u32[]{:S(2)}) collective-permute-start(bf16[192,1024]{1,0:T(8,128)(2,1)S(1)} %collective-permute-done.11), channel_id=1, source_target_pairs={{0,1},{1,2},{2,3},{3,4},{4,5},{5,6},{6,7},{7,0},{8,9},{9,10},{10,1... | collective-permute-start | bytes 1179656 | tf_op jit(solution)/shard_map/ppermute | solution.py:214
  261.3 10.9 %collective-permute-start.13 = (bf16[96,1024]{1,0:T(8,128)(2,1)S(1)}, bf16[96,1024]{1,0:T(8,128)(2,1)S(1)}, u32[]{:S(2)}, u32[]{:S(2)}) collective-permute-start(bf16[96,1024]{1,0:T(8,128)(2,1)S(1)} %slice.62), channel_id=1, source_target_pairs={{0,1},{1,2},{2,3},{3,4},{4,5},{5,6},{6,7},{7,0},{8,9},{9,10},{10,1... | collective-permute-start | bytes 589832 | tf_op jit(solution)/shard_map/ppermute | solution.py:219
  261.5 10.7 %collective-permute-start.14 = (bf16[96,1024]{1,0:T(8,128)(2,1)S(1)}, bf16[96,1024]{1,0:T(8,128)(2,1)S(1)}, u32[]{:S(2)}, u32[]{:S(2)}) collective-permute-start(bf16[96,1024]{1,0:T(8,128)(2,1)S(1)} %slice.63), channel_id=1, source_target_pairs={{0,7},{1,0},{2,1},{3,2},{4,3},{5,4},{6,5},{7,6},{8,15},{9,8},{10,9... | collective-permute-start | bytes 589832 | tf_op jit(solution)/shard_map/ppermute | solution.py:220
  272.4 9.8 %copy-start.11 = (bf16[1,1536,512]{2,1,0:T(8,128)(2,1)S(1)}, bf16[1,1536,512]{2,1,0:T(8,128)(2,1)}, u32[]{:S(2)}) copy-start(bf16[1,1536,512]{2,1,0:T(8,128)(2,1)} %param.13) | copy-start | bytes 4718596
  286.9 37.7 %copy-start.2 = (bf16[1024,512]{1,0:T(8,128)(2,1)S(1)}, bf16[1024,512]{1,0:T(8,128)(2,1)}, u32[]{:S(2)}) copy-start(bf16[1024,512]{1,0:T(8,128)(2,1)} %select_convert_fusion) | copy-start | bytes 3145732
  286.9 37.6 %copy-start.3 = (bf16[1024,512]{1,0:T(8,128)(2,1)S(1)}, bf16[1024,512]{1,0:T(8,128)(2,1)}, u32[]{:S(2)}) copy-start(bf16[1024,512]{1,0:T(8,128)(2,1)} %select_convert_fusion.1) | copy-start | bytes 3145732
  286.9 37.6 %copy-start.5 = (bf16[1024,256]{1,0:T(8,128)(2,1)S(1)}, bf16[1024,256]{1,0:T(8,128)(2,1)}, u32[]{:S(2)}) copy-start(bf16[1024,256]{1,0:T(8,128)(2,1)} %fusion.11.last_high) | copy-start | bytes 1572868
  324.5 38.7 %copy-start.1 = (f32[4096,128]{1,0:T(8,128)S(1)}, f32[4096,128]{1,0:T(8,128)}, u32[]{:S(2)}) copy-start(f32[4096,128]{1,0:T(8,128)} %param.8) | copy-start | bytes 6291460
Sparse Core Ops, SparseCore 0:
  9.1 45.4 all-gather.4
  61.6 134.8 all-gather.8
  210.1 72.0 all-gather.6
